TPU v7x, 32 devices: a whole 2x2x4 slice. The times are simulated.
32 devices in a mesh: grp: 2 (over x), req: 16 (over z, y, core).
Axes of the slice: x: 2, y: 2, z: 4, core: 2. Of those that a mesh axis runs over, the one named last changes fastest.
Arguments:
- xbc: bfloat16 [4096, 9216], P(('grp', 'req')), parts along dimension 0, may hold values from -6 to 6
- dt_raw: float32 [4096, 128], P(('grp', 'req')), parts along dimension 0, may hold values from -6 to 6
- conv_weight: float32 [4, 9216], replicated, may hold values from -3 to 3
- conv_bias: float32 [9216], replicated, may hold values from -3 to 3
- dt_bias: float32 [128], replicated, may hold values from -1 to 1
- a_log: float32 [128], replicated, may hold values from -6 to -2.5
- d_skip: float32 [128], replicated, may hold values from 0.5 to 1.5
- cache_states: bfloat16 [96, 128, 8192], P(('grp', 'req')), parts along dimension 0, may hold values from -24 to 24
- cache_tails: bfloat16 [96, 3, 9216], P(('grp', 'req')), parts along dimension 0, may hold values from -6 to 6
- hit_owner: int32 [32], P('grp'), parts along dimension 0, may hold values from 0 to 15, as said below
- hit_slot: int32 [32], P('grp'), parts along dimension 0, may hold values from 0 to 2, as said below
- hit_spans: int32 [32], P('grp'), parts along dimension 0, may hold values from 0 to 4
- request_of: int32 [32], P(('grp', 'req')), parts along dimension 0, may hold values from 0 to 15, each once
Outputs:
- y_out: bfloat16 [4096, 8192], P(('grp', 'req')), parts along dimension 0
- final_state: bfloat16 [32, 128, 8192], P(('grp', 'req')), parts along dimension 0
There are 2 independent parts, one for each index of `grp`. A program takes and returns all parts, laid end to end along the dimension named above; an argument that names none is the same for every part. Nothing has to cross between parts.
Inputs may be any that keep to these rules, and one draw needn't show every extreme that they name: `hit_owner`: owners are skewed: some devices hold the prefixes of several requests, others of none. `hit_slot`: all requests that name the same owner device name the same slot of it. `request_of`: each request stands on exactly one device.
All inputs are finite; a program needn't handle non-finite values.
Results may differ from a plain program's by a relative error of at most 0.0039.
Values may be sent and summed in bfloat16 or wider, within the bound.
A program may use at most 128 MiB of HBM per device.

v0:
```python
import jax
import jax.numpy as jnp
from jax import lax
from jax.sharding import PartitionSpec as P

HEADS = 128
HEAD_DIM = 64
GROUPS = 4
NST = 128
INNER = 8192


def convolve(xrows, tail, conv_weight, conv_bias):
    rows = xrows.shape[0]
    taps = conv_weight.shape[0]
    extended = jnp.concatenate([tail, xrows], axis=0).astype(jnp.float32)
    conv = jnp.zeros((rows, xrows.shape[1]), jnp.float32) + conv_bias[None, :]
    for k in range(taps):
        conv = conv + conv_weight[k][None, :] * extended[k : k + rows]
    return jax.nn.silu(conv).astype(jnp.bfloat16)


def local_part(conv_out, dt_rows, dt_bias, a_log, d_skip):
    rows = conv_out.shape[0]
    per_group = HEADS // GROUPS
    inputs = conv_out[:, :INNER].reshape(rows, GROUPS, per_group, HEAD_DIM)
    b_part = conv_out[:, INNER : INNER + GROUPS * NST].reshape(rows, GROUPS, NST)
    c_part = conv_out[:, INNER + GROUPS * NST :].reshape(rows, GROUPS, NST)
    step = jax.nn.softplus(dt_rows + dt_bias[None, :])
    cum = jnp.cumsum(step * (-jnp.exp(a_log))[None, :], axis=0)
    scores = jnp.einsum("tgn,sgn->gts", c_part, b_part, preferred_element_type=jnp.float32)
    diff = cum.T[:, :, None] - cum.T[:, None, :]
    causal = lax.broadcasted_iota(jnp.int32, (rows, rows), 0) >= lax.broadcasted_iota(
        jnp.int32, (rows, rows), 1
    )
    decay = jnp.where(causal[None], jnp.exp(jnp.minimum(diff, 0.0)), 0.0)
    mixing = (
        scores[:, None]
        * decay.reshape(GROUPS, per_group, rows, rows)
        * step.T.reshape(GROUPS, per_group, 1, rows)
    ).astype(jnp.bfloat16)
    y_intra = jnp.einsum("gjts,sgjp->tgjp", mixing, inputs, preferred_element_type=jnp.float32)
    y_local = y_intra + d_skip.reshape(1, GROUPS, per_group, 1) * inputs.astype(jnp.float32)
    last = cum[rows - 1]
    carried = (
        (jnp.exp(last[None, :] - cum) * step).reshape(rows, GROUPS, per_group, 1)
        * inputs.astype(jnp.float32)
    ).astype(jnp.bfloat16)
    fresh = jnp.einsum("sgn,sgjp->ngjp", b_part, carried, preferred_element_type=jnp.float32)
    return (y_local, fresh, c_part, cum)


def state_part(start, c_part, cum):
    rows = c_part.shape[0]
    per_group = HEADS // GROUPS
    start_view = start.reshape(NST, GROUPS, per_group, HEAD_DIM)
    y_state = jnp.einsum("tgn,ngjp->tgjp", c_part, start_view, preferred_element_type=jnp.float32)
    y_state = y_state * jnp.exp(cum).reshape(rows, GROUPS, per_group, 1)
    kept = jnp.exp(cum[rows - 1]).reshape(1, GROUPS, per_group, 1) * start_view.astype(jnp.float32)
    return (y_state, kept)


def local(
    xbc,
    dt_raw,
    conv_weight,
    conv_bias,
    dt_bias,
    a_log,
    d_skip,
    cache_states,
    cache_tails,
    hit_owner,
    hit_slot,
    hit_spans,
    request_of,
):
    slots = cache_states.shape[0]
    every_request = lax.all_gather(request_of, "req", axis=0, tiled=True)
    mine = request_of[0]
    own_row = hit_owner[mine] * slots + hit_slot[mine]
    live = hit_spans[mine] > 0
    device = lax.axis_index("req")
    served = jnp.max(jnp.where(hit_owner == device, hit_slot, 0))
    send_states = lax.dynamic_slice_in_dim(cache_states, served, 1, 0)
    wanted_rows = hit_owner[every_request]
    every_tail = lax.all_gather(cache_tails, "req", axis=0, tiled=True)
    tail = lax.dynamic_index_in_dim(every_tail, own_row, 0, keepdims=False)
    state_parts = lax.all_to_all(send_states, "req", split_axis=2, concat_axis=0, tiled=True)
    state_chosen = jnp.take(state_parts, wanted_rows, axis=0)
    start = lax.all_to_all(state_chosen, "req", split_axis=0, concat_axis=2, tiled=True)[0]
    tail = jnp.where(live, tail, jnp.zeros_like(tail))
    start = jnp.where(live, start, jnp.zeros_like(start))
    conv_out = convolve(xbc, tail, conv_weight, conv_bias)
    y_local, fresh, c_part, cum = local_part(conv_out, dt_raw, dt_bias, a_log, d_skip)
    y_state, kept = state_part(start, c_part, cum)
    rows = xbc.shape[0]
    y_out = (y_local + y_state).reshape(rows, INNER).astype(jnp.bfloat16)
    final_state = (kept + fresh).reshape(1, NST, INNER).astype(jnp.bfloat16)
    return (y_out, final_state)


def solution(mesh):
    in_specs = (
        P(("grp", "req"), None),
        P(("grp", "req"), None),
        P(),
        P(),
        P(),
        P(),
        P(),
        P(("grp", "req"), None, None),
        P(("grp", "req"), None, None),
        P("grp"),
        P("grp"),
        P("grp"),
        P(("grp", "req")),
    )
    out_specs = (P(("grp", "req"), None), P(("grp", "req"), None, None))
    return jax.shard_map(local, mesh=mesh, in_specs=in_specs, out_specs=out_specs, check_vma=False)
```

profile of v0, /device:TPU:13, one launch (start us, length us, event | category | flops | bytes accessed | tf_op | source)
XLA Modules:
  0.0 240.6 jit_solution(13793065196203515922)
XLA Ops:
  7.9 1.2 dynamic-slice
  9.1 0.8 dynamic-update-slice
  9.9 7.9 %all-reduce = s32[16]{0:T(128)S(1)} all-reduce(s32[16]{0:T(128)S(1)} %dynamic-update-slice), channel_id=1, replica_groups=mesh['grp'=2,'req'=16] {'req'}, use_global_device_ids=true, to_apply=%add | all-reduce | flops 16 | bytes 128
  17.8 1.3 compare_select_fusion.3
  21.1 1.7 constant_dynamic-slice_fusion
  22.8 6.9 %copy.73 = bf16[1,128,8192]{1,0,2:T(2,128)(2,1)} copy(bf16[1,128,8192]{2,1,0:T(8,128)(2,1)S(1)} %constant_dynamic-slice_fusion) | data formatting | bytes 4194304
  30.2 45.2 %reduce.4 = bf16[8192,128]{1,0:T(8,128)(2,1)S(1)} reduce(bf16[8192,1,128]{2,1,0:T(2,128)(2,1)} %bitcast.66, bf16[]{:T(256)} %broadcast.94), dimensions={1}, to_apply=%bitcast.55.reduce_sub_computation | reduce | bytes 4194306
  75.4 2.0 reshape.136
  77.4 9.4 %all-to-all-start = ((bf16[16,2,32768]{2,1,0:T(2,128)(2,1)}), bf16[16,2,32768]{2,1,0:T(2,128)(2,1)}, u32[]{:S(2)}, u32[]{:S(2)}) async-start(bf16[16,2,32768]{2,1,0:T(2,128)(2,1)} %reshape.136), calls=%async_computation | async-start | bytes 4194304 | tf_op jit(solution)/shard_map/all_to_all | solution.py:89
  90.1 3.0 %copy.50 = bf16[128,9216]{0,1:T(8,128)(2,1)S(1)} copy(bf16[128,9216]{1,0:T(8,128)(2,1)} %param.13) | data formatting | bytes 4718592 | tf_op args[0]
  93.2 0.7 gather_fusion
  95.7 38.7 %all-to-all-done = bf16[16,2,32768]{2,1,0:T(2,128)(2,1)} async-done(((bf16[16,2,32768]{2,1,0:T(2,128)(2,1)}), bf16[16,2,32768]{2,1,0:T(2,128)(2,1)}, u32[]{:S(2)}, u32[]{:S(2)}) %all-to-all-start) | async-done | bytes 2097184 | tf_op jit(solution)/shard_map/all_to_all | solution.py:89
  134.4 10.4 %reshape.137 = bf16[8192,1,128]{2,1,0:T(2,128)(2,1)} reshape(bf16[16,2,32768]{2,1,0:T(2,128)(2,1)} %all-to-all-done) | data formatting | bytes 4194304
  144.8 3.8 %copy.72 = bf16[1,128,8192]{1,2,0:T(8,128)(2,1)} copy(bf16[1,128,8192]{1,0,2:T(2,128)(2,1)} %bitcast.67) | data formatting | bytes 4194304
  148.6 3.9 %copy.56 = bf16[1,128,16,512]{3,1,2,0:T(8,128)(2,1)} copy(bf16[1,128,16,512]{1,3,2,0:T(8,128)(2,1)} %bitcast.68) | data formatting | bytes 4194304 | tf_op jit(solution)/shard_map/all_to_all | solution.py:89
  152.5 3.6 %gather_fusion.1 = bf16[16,128,512]{2,1,0:T(8,128)(2,1)} fusion(bf16[16,128,512]{2,1,0:T(8,128)(2,1)} %bitcast.69, s32[1024]{0:T(1024)S(1)} %pad_clamp_fusion), kind=kCustom, calls=%fused_computation.1 | custom fusion | bytes 4194368 | tf_op jit(solution)/shard_map/jit(_take)/gather | solution.py:90
  156.1 3.2 %broadcast_select_fusion = bf16[16,128,512]{2,1,0:T(8,128)(2,1)} fusion(bf16[16,128,512]{2,1,0:T(8,128)(2,1)} %gather_fusion.1, pred[16]{0:T(512)(128)(4,1)S(1)} %compare_and_fusion), kind=kLoop, calls=%fused_computation.32 | loop fusion | flops 1048576 | bytes 4194320 | tf_op jit(solution)/shard_map/jit(_take)/select_n | solution.py:90
  159.2 4.9 %all-to-all-start.1 = ((bf16[16,128,512]{2,1,0:T(8,128)(2,1)}), bf16[16,128,512]{2,1,0:T(8,128)(2,1)}, u32[]{:S(2)}, u32[]{:S(2)}) async-start(bf16[16,128,512]{2,1,0:T(8,128)(2,1)} %broadcast_select_fusion), calls=%async_computation.1 | async-start | bytes 4194304 | tf_op jit(solution)/shard_map/all_to_all | solution.py:91
  164.2 0.9 constant_dynamic-slice_fusion.1
  165.1 2.0 copy.74
  167.1 1.7 select_bitcast_fusion
  168.8 1.8 maximum_convert_fusion
  170.7 11.8 %multiply_convert_fusion.1 = bf16[128,9216]{0,1:T(8,128)(2,1)S(1)} fusion(f32[131,9216]{0,1:T(8,128)S(1)} %maximum_convert_fusion, f32[9216]{0:T(1024)S(1)} %bitcast.85, f32[9216]{0:T(1024)S(1)} %bitcast.86, f32[9216]{0:T(1024)S(1)} %bitcast.84, f32[9216]{0:T(1024)S(1)} %bitcast.83, f32[9216]{0:T(1024)S(1)} %copy-done.5), kind=kLoop, calls=%fused_computation.14 | loop fusion | flops 15335424 | bytes 21417984 | tf_op jit(solution)/shard_map/convert_element_type | solution.py:20
  182.9 1.0 copy-done.1
  183.9 6.0 %fusion.4 = f32[4,32,64,128]{3,2,1,0:T(8,128)} fusion(bf16[128,4,32,64]{0,3,2,1:T(8,128)(2,1)S(1)} %bitcast.70, f32[4,32,128]{2,1,0:T(8,128)S(1)} %bitcast.88, f32[4,32,128]{2,1,0:T(8,128)S(1)} %bitcast.89, f32[4,128,128]{2,1,0:T(8,128)S(1)} %fusion.24, pred[128,128]{1,0:T(8,128)(4,1)S(1)} %iota_compare_fusion), kind=kOutput, calls=%fused_computation.15 | convolution fusion | flops 281018368 | bytes 6701056 | tf_op jit(solution)/shard_map/gjts,sgjp->tgjp/dot_general | solution.py:42
  189.9 21.7 %all-to-all-done.1 = bf16[16,128,512]{2,1,0:T(8,128)(2,1)} async-done(((bf16[16,128,512]{2,1,0:T(8,128)(2,1)}), bf16[16,128,512]{2,1,0:T(8,128)(2,1)}, u32[]{:S(2)}, u32[]{:S(2)}) %all-to-all-start.1) | async-done | bytes 2097184 | tf_op jit(solution)/shard_map/all_to_all | solution.py:91
  211.7 1.7 select_bitcast_fusion.1
  213.4 2.4 copy.57
  215.8 4.7 %fusion.9 = bf16[128,4,32,64]{0,3,2,1:T(8,128)(2,1)} fusion(bf16[128,4,32,64]{0,3,2,1:T(8,128)(2,1)} %bitcast.73, bf16[128,4,128,1]{0,2,3,1:T(8,128)(2,1)S(1)} %bitcast.81, bf16[128,4,32,64]{0,3,2,1:T(8,128)(2,1)} %bitcast.71, f32[128,4,32]{0,2,1:T(8,128)S(1)} %bitcast.87, f32[4,32]{1,0:T(4,128)S(1)} %exp.45), kind=kOutput, calls=%fused_computation.21 | convolution fusion | flops 275775488 | bytes 6488576 | tf_op jit(solution)/shard_map/sgn,sgjp->ngjp/dot_general | solution.py:49
  220.5 4.1 %copy.63 = bf16[1,128,8192]{2,1,0:T(8,128)(2,1)} copy(bf16[1,128,8192]{1,2,0:T(8,128)(2,1)} %bitcast.76) | data formatting | bytes 4194304
  224.5 5.2 %fusion.7 = bf16[128,4,32,64]{0,3,2,1:T(8,128)(2,1)} fusion(bf16[128,4,32,64]{0,3,2,1:T(8,128)(2,1)S(1)} %bitcast.72, f32[4,32,64,128]{3,2,1,0:T(8,128)} %fusion.4, bf16[128,4,32,64]{0,3,2,1:T(8,128)(2,1)} %bitcast.74, bf16[128,4,128,1]{0,2,3,1:T(8,128)(2,1)S(1)} %bitcast.78, f32[128,4,32]{0,2,1:T(8,128)S(1)} %bitcast.82, f32[4,32]{1,0:T(4,128)S(1)} %mul.134), kind=kOutput, calls=%fused_computation.18 | convolution fusion | flops 274726912 | bytes 10682880 | tf_op jit(solution)/shard_map/tgn,ngjp->tgjp/dot_general | solution.py:57
  229.7 4.1 %copy.62 = bf16[128,8192]{1,0:T(8,128)(2,1)} copy(bf16[128,8192]{0,1:T(8,128)(2,1)} %bitcast.75) | data formatting | bytes 4194304
  (49 shorter events, 3.9 us)
Async XLA Ops:
  7.2 157.0 %all-gather.2.cloned.1.call-start = ((), (), s32[]{:S(2)}) async-start(), calls=%async_computation.2 | async-start | bytes 3760128 | tf_op jit(solution)/shard_map/all_gather | solution.py:87
  75.4 11.5 %copy-start = (s32[16]{0:T(128)S(1)}, s32[16]{0:T(128)}, u32[]{:S(2)}) copy-start(s32[16]{0:T(128)} %param.22) | copy-start | bytes 196
  75.4 12.1 %copy-start.8 = (s32[16]{0:T(128)S(1)}, s32[16]{0:T(128)}, u32[]{:S(2)}) copy-start(s32[16]{0:T(128)} %param.23) | copy-start | bytes 196
  75.4 14.1 %copy-start.9 = (s32[16]{0:T(128)S(1)}, s32[16]{0:T(128)}, u32[]{:S(2)}) copy-start(s32[16]{0:T(128)} %param.24) | copy-start | bytes 196
  77.4 16.4 %copy-start.10 = (f32[128]{0:T(128)S(1)}, f32[128]{0:T(128)}, u32[]{:S(2)}) copy-start(f32[128]{0:T(128)} %param.18) | copy-start | bytes 1540
  77.4 16.5 %copy-start.3 = (f32[128,128]{1,0:T(8,128)S(1)}, f32[128,128]{1,0:T(8,128)}, u32[]{:S(2)}) copy-start(f32[128,128]{1,0:T(8,128)} %param.14) | copy-start | bytes 196612
  77.4 16.5 %copy-start.6 = (f32[128]{0:T(128)S(1)}, f32[128]{0:T(128)}, u32[]{:S(2)}) copy-start(f32[128]{0:T(128)} %param.17) | copy-start | bytes 1540
  77.4 57.0 %all-to-all-start = ((bf16[16,2,32768]{2,1,0:T(2,128)(2,1)}), bf16[16,2,32768]{2,1,0:T(2,128)(2,1)}, u32[]{:S(2)}, u32[]{:S(2)}) async-start(bf16[16,2,32768]{2,1,0:T(2,128)(2,1)} %reshape.136), calls=%async_computation | async-start | bytes 4194304 | tf_op jit(solution)/shard_map/all_to_all | solution.py:89
  86.9 7.8 %copy-start.7 = (f32[128]{0:T(128)S(1)}, f32[128]{0:T(128)}, u32[]{:S(2)}) copy-start(f32[128]{0:T(128)} %param.19) | copy-start | bytes 1540
  86.9 8.7 %copy-start.4 = (f32[4,9216]{1,0:T(4,128)S(1)}, f32[4,9216]{1,0:T(4,128)}, u32[]{:S(2)}) copy-start(f32[4,9216]{1,0:T(4,128)} %param.15) | copy-start | bytes 442372
  159.2 52.4 %all-to-all-start.1 = ((bf16[16,128,512]{2,1,0:T(8,128)(2,1)}), bf16[16,128,512]{2,1,0:T(8,128)(2,1)}, u32[]{:S(2)}, u32[]{:S(2)}) async-start(bf16[16,128,512]{2,1,0:T(8,128)(2,1)} %broadcast_select_fusion), calls=%async_computation.1 | async-start | bytes 4194304 | tf_op jit(solution)/shard_map/all_to_all | solution.py:91
  168.8 1.8 copy-start.5
  182.6 1.3 copy-start.1
  215.8 8.8 %copy-start.2 = (bf16[128,8192]{0,1:T(8,128)(2,1)S(1)}, bf16[128,8192]{0,1:T(8,128)(2,1)}, u32[]{:S(2)}) copy-start(bf16[128,8192]{0,1:T(8,128)(2,1)} %copy-done.1) | copy-start | bytes 6291460
Sparse Core Ops, SparseCore 0:
  10.3 48.3 all-gather.1
where the time goes:
time: 242 us; the launch traced here: 241 us
  other arithmetic  67 us (28%)
  waiting for transfers between devices  60.5 us (25%)
  local copies, waits for them, and re-layouts  55.7 us (23%)
  between operations  19 us (8%)
  matrix products  16.1 us (7%)
  starting transfers between devices  14.4 us (6%)
  blocking collectives  7.91 us (3%)
    unnamed x1, other arithmetic  45.2 us
    unnamed x34, local copies, waits for them, and re-layouts  39.9 us
    all_to_all x1, waiting for transfers between devices, local(): lax.all_to_all(send_states, 'req', split_axis=2, concat_axis=0, tiled=True)  38.7 us
    all_to_all x1, waiting for transfers between devices, local(): lax.all_to_all(state_chosen, 'req', split_axis=0, concat_axis=2, tiled=True)  21.7 us
    convert_element_type x1, other arithmetic, convolve(): return jax.nn.silu(conv).astype(jnp.bfloat16)  11.8 us
    all_to_all x1, starting transfers between devices, local(): lax.all_to_all(send_states, 'req', split_axis=2, concat_axis=0, tiled=True)  9.43 us
    unnamed x1, blocking collectives  7.91 us
    dot_general x1, matrix products, local_part(): jnp.einsum('gjts,sgjp->tgjp', mixing, inputs, preferred_element_type=jnp....  5.99 us
  transfers between devices with their start and end apart: 3, of which 2 were waited for; matrix products, arithmetic and copies ran while one was open for 47% of the time, Pallas kernels for 0%

commit v1 on v0

v1 whole, which is shorter than its diff:
```python
import jax
import jax.numpy as jnp
from jax import lax
from jax.experimental import pallas as pl
from jax.experimental.pallas import tpu as pltpu
from jax.sharding import PartitionSpec as P

HEADS = 128
HEAD_DIM = 64
GROUPS = 4
NST = 128
INNER = 8192
PER_STEP = 16
COLS = PER_STEP * HEAD_DIM
STEPS = HEADS // PER_STEP
STEPS_PER_GROUP = STEPS // GROUPS


def pick_kernel(index_ref, parts_ref, out_ref, sem):
    count = out_ref.shape[0]
    copies = []
    for i in range(count):
        copy = pltpu.make_async_copy(parts_ref.at[index_ref[i]], out_ref.at[i], sem.at[i])
        copy.start()
        copies.append(copy)
    for copy in copies:
        copy.wait()


def pick(parts, index):
    count = index.shape[0]
    return pl.pallas_call(
        pick_kernel,
        out_shape=jax.ShapeDtypeStruct((count,) + parts.shape[1:], parts.dtype),
        in_specs=[pl.BlockSpec(memory_space=pltpu.SMEM), pl.BlockSpec(memory_space=pl.ANY)],
        out_specs=pl.BlockSpec(memory_space=pl.ANY),
        scratch_shapes=[pltpu.SemaphoreType.DMA((count,))],
        name="pick",
    )(index, parts)


def conv_block(pad, x_ref, tail_ref, w_ref, b_ref, width):
    rows = x_ref.shape[0]
    pad[0:8, 0:width] = tail_ref[...]
    pad[8 : 8 + rows, 0:width] = x_ref[...].astype(jnp.float32)
    v = jnp.broadcast_to(b_ref[...], (rows, width))
    for k in range(4):
        v = v + w_ref[k : k + 1, :] * pad[5 + k : 5 + k + rows, 0:width]
    return (v / (1.0 + jnp.exp(-v))).astype(jnp.bfloat16)


def local_kernel(
    x_ref, xb_ref, xc_ref, tx_ref, tb_ref, tc_ref, wx_ref, wb_ref, wc_ref, bx_ref, bb_ref, bc_ref,
    cum_ref, cumt_ref, stept_ref, coef_ref, skip_ref,
    y_ref, fresh_ref, c_out_ref, pad,
):
    rows = x_ref.shape[0]
    b_part = conv_block(pad, xb_ref, tb_ref, wb_ref, bb_ref, NST)
    c_part = conv_block(pad, xc_ref, tc_ref, wc_ref, bc_ref, NST)
    c_out_ref[...] = c_part
    x = conv_block(pad, x_ref, tx_ref, wx_ref, bx_ref, COLS)
    scores = lax.dot_general(c_part, b_part, (((1,), (1,)), ((), ())), preferred_element_type=jnp.float32)
    causal = lax.broadcasted_iota(jnp.int32, (rows, rows), 0) >= lax.broadcasted_iota(jnp.int32, (rows, rows), 1)
    scores = jnp.where(causal, scores, 0.0)
    low = lax.broadcasted_iota(jnp.int32, (rows, 128), 1) < HEAD_DIM
    cum = cum_ref[0]
    coef = coef_ref[0]
    zero = jnp.zeros((rows, 128), jnp.bfloat16)
    carried = []
    for j in range(0, PER_STEP, 2):
        xp = x[:, j * HEAD_DIM : (j + 2) * HEAD_DIM]
        mixes = []
        for h in (j, j + 1):
            decay = jnp.exp(jnp.minimum(cum[:, h : h + 1] - cumt_ref[0, h : h + 1, :], 0.0))
            mixes.append((scores * decay * stept_ref[0, h : h + 1, :]).astype(jnp.bfloat16))
        mix = jnp.concatenate(mixes, axis=1)
        both = jnp.concatenate([jnp.where(low, xp, zero), jnp.where(low, zero, xp)], axis=0)
        xf = xp.astype(jnp.float32)
        sl = slice(j * HEAD_DIM, (j + 2) * HEAD_DIM)
        y_ref[:, sl] = jnp.dot(mix, both, preferred_element_type=jnp.float32) + skip_ref[:, sl] * xf
        carried.append((jnp.where(low, coef[:, j : j + 1], coef[:, j + 1 : j + 2]) * xf).astype(jnp.bfloat16))
    fresh_ref[...] = lax.dot_general(
        b_part, jnp.concatenate(carried, axis=1), (((0,), (0,)), ((), ())), preferred_element_type=jnp.float32
    )


def state_kernel(live_ref, start_ref, y_ref, fresh_ref, c_ref, ecum_ref, elast_ref, y_out_ref, final_ref):
    rows = y_ref.shape[0]
    start = start_ref[...]
    start = jnp.where(live_ref[0] > 0, start, jnp.zeros_like(start))
    low = lax.broadcasted_iota(jnp.int32, (rows, 128), 1) < HEAD_DIM
    ecum = ecum_ref[0]
    ys = jnp.dot(c_ref[...], start, preferred_element_type=jnp.float32)
    for j in range(0, PER_STEP, 2):
        sl = slice(j * HEAD_DIM, (j + 2) * HEAD_DIM)
        factor = jnp.where(low, ecum[:, j : j + 1], ecum[:, j + 1 : j + 2])
        y_out_ref[:, sl] = (y_ref[:, sl] + factor * ys[:, sl]).astype(jnp.bfloat16)
    final_ref[0] = (elast_ref[...] * start.astype(jnp.float32) + fresh_ref[...]).astype(jnp.bfloat16)


def by_step(a):
    return a.reshape(a.shape[0], STEPS, PER_STEP).transpose(1, 0, 2)


def local(
    xbc, dt_raw, conv_weight, conv_bias, dt_bias, a_log, d_skip, cache_states, cache_tails,
    hit_owner, hit_slot, hit_spans, request_of,
):
    count = hit_owner.shape[0]
    rows = xbc.shape[0]
    mine = request_of[0]
    live = (hit_spans[mine] > 0).astype(jnp.int32)
    device = lax.axis_index("req")
    served = jnp.max(jnp.where(hit_owner == device, hit_slot, 0))
    send = lax.dynamic_slice_in_dim(cache_states, served, 1, 0).reshape(count, NST // count, INNER)
    parts = lax.all_to_all(send, "req", split_axis=0, concat_axis=0, tiled=True)

    own_tail = lax.dynamic_slice_in_dim(cache_tails, served, 1, 0)
    every_tail = lax.all_gather(own_tail, "req", axis=0, tiled=True)
    every_request = lax.all_gather(request_of, "req", axis=0, tiled=True)
    chosen = pick(parts, hit_owner[every_request])
    start = lax.all_to_all(chosen, "req", split_axis=0, concat_axis=0, tiled=True).reshape(NST, INNER)

    tail = lax.dynamic_index_in_dim(every_tail, hit_owner[mine], 0, keepdims=False)
    tail = jnp.where(live > 0, tail, jnp.zeros_like(tail)).astype(jnp.float32)
    tail = jnp.pad(tail, ((5, 0), (0, 0)))
    step = jax.nn.softplus(dt_raw + dt_bias[None, :])
    below = jnp.tril(jnp.ones((rows, rows), jnp.float32))
    cum = jnp.dot(below, step * (-jnp.exp(a_log))[None, :], precision=lax.Precision.HIGHEST)
    last = cum[rows - 1]
    coef = jnp.exp(last[None, :] - cum) * step
    skip = jnp.repeat(d_skip, HEAD_DIM)[None, :]
    elast = jnp.repeat(jnp.exp(last), HEAD_DIM)[None, :]
    cumt = cum.T.reshape(STEPS, PER_STEP, rows)
    stept = step.T.reshape(STEPS, PER_STEP, rows)
    bias = conv_bias[None, :]

    first_b, first_c = INNER // NST, INNER // NST + GROUPS
    per = STEPS_PER_GROUP
    triple = lambda r: [
        pl.BlockSpec((r, COLS), lambda i: (0, i)),
        pl.BlockSpec((r, NST), lambda i: (0, first_b + i // per)),
        pl.BlockSpec((r, NST), lambda i: (0, first_c + i // per)),
    ]
    wide = lambda r: pl.BlockSpec((r, COLS), lambda i: (0, i))
    tall = pl.BlockSpec((1, rows, PER_STEP), lambda i: (i, 0, 0))
    flat = pl.BlockSpec((1, PER_STEP, rows), lambda i: (i, 0, 0))
    group = pl.BlockSpec((rows, NST), lambda i: (0, i // per))
    y_local, fresh, c_part = pl.pallas_call(
        local_kernel,
        grid=(STEPS,),
        out_shape=(
            jax.ShapeDtypeStruct((rows, INNER), jnp.float32),
            jax.ShapeDtypeStruct((NST, INNER), jnp.float32),
            jax.ShapeDtypeStruct((rows, GROUPS * NST), jnp.bfloat16),
        ),
        in_specs=triple(rows) + triple(8) + triple(4) + triple(1) + [tall, flat, flat, tall, wide(1)],
        out_specs=(wide(rows), wide(NST), group),
        scratch_shapes=[pltpu.VMEM((8 + rows, COLS), jnp.float32)],
        compiler_params=pltpu.CompilerParams(vmem_limit_bytes=40 * 2**20),
        cost_estimate=pl.CostEstimate(flops=10**9, bytes_accessed=40 * 10**6, transcendentals=4 * 10**6),
        name="local",
    )(xbc, xbc, xbc, tail, tail, tail, conv_weight, conv_weight, conv_weight, bias, bias, bias,
      by_step(cum), cumt, stept, by_step(coef), skip)

    return pl.pallas_call(
        state_kernel,
        grid=(STEPS,),
        out_shape=(
            jax.ShapeDtypeStruct((rows, INNER), jnp.bfloat16),
            jax.ShapeDtypeStruct((1, NST, INNER), jnp.bfloat16),
        ),
        in_specs=[pl.BlockSpec(memory_space=pltpu.SMEM), wide(NST), wide(rows), wide(NST), group, tall, wide(1)],
        out_specs=(wide(rows), pl.BlockSpec((1, NST, COLS), lambda i: (0, 0, i))),
        compiler_params=pltpu.CompilerParams(vmem_limit_bytes=40 * 2**20),
        name="state",
    )(live[None], start, y_local, fresh, c_part, by_step(jnp.exp(cum)), elast)


def solution(mesh):
    rows = P(("grp", "req"), None)
    slots = P(("grp", "req"), None, None)
    in_specs = (
        rows, rows, P(), P(), P(), P(), P(), slots, slots, P("grp"), P("grp"), P("grp"), P(("grp", "req")),
    )
    return jax.shard_map(local, mesh=mesh, in_specs=in_specs, out_specs=(rows, slots), check_vma=False)
```

time: 242 us -> 237 us (0.979)
  Pallas kernels: 0 us -> 84.1 us
  other arithmetic: 67 us -> 1.63 us
  blocking collectives: 7.91 us -> 60.5 us
  local copies, waits for them, and re-layouts: 55.7 us -> 22.8 us
  matrix products: 16.1 us -> 0.25 us
  waiting for transfers between devices: 60.5 us -> 45.9 us
  between operations: 19 us -> 6.12 us
    pallas_call x0 -> x3, Pallas kernels: none -> 84.1 us  [the longest x1 65.4 us: pick(): pl.pallas_call(pick_kernel, out_shape=jax.ShapeDtypeStruct((count,) + par...]
    all_gather x0 -> x1, blocking collectives: none -> 52.7 us  [local(): every_tail = lax.all_gather(own_tail, 'req', axis=0, tiled=True)]
    unnamed x1 -> x0, other arithmetic: 45.2 us -> none
    unnamed x34 -> x42, local copies, waits for them, and re-layouts: 39.9 us -> 13.3 us
    dot_general x4 -> x1, matrix products: 16.1 us -> 0.25 us  [local(): jnp.dot(below, step * (-jnp.exp(a_log))[None, :], precision=lax.Precision...]
    all_to_all x2, waiting for transfers between devices: 60.5 us -> 45.9 us  [the longest x1 45.9 us: local(): parts = lax.all_to_all(send, 'req', split_axis=0, concat_axis=0, tiled=True)]
    convert_element_type x2 -> x1, other arithmetic: 13.6 us -> 0.04 us  [local(): tail = jnp.where(live > 0, tail, jnp.zeros_like(tail)).astype(jnp.float32)]
    select_n x5 -> x2, other arithmetic: 7.94 us -> 1.42 us  [the longest x1 1.31 us: local(): chosen = pick(parts, hit_owner[every_request])]
  transfers between devices with their start and end apart: 3 -> 2, of which waited for: 2 -> 1; matrix products, arithmetic and copies ran while one was open for 47% -> 3% of each run, Pallas kernels for 0% -> 5%
where the time goes in v1:
time: 237 us; the launch traced here: 235 us
  Pallas kernels  84.1 us (35%)
  blocking collectives  60.5 us (26%)
  waiting for transfers between devices  45.9 us (19%)
  local copies, waits for them, and re-layouts  22.8 us (10%)
  starting transfers between devices  13.7 us (6%)
  between operations  6.12 us (3%)
    pallas_call x1, Pallas kernels, pick(): pl.pallas_call(pick_kernel, out_shape=jax.ShapeDtypeStruct((count,) + par...  65.4 us
    all_gather x1, blocking collectives, local(): every_tail = lax.all_gather(own_tail, 'req', axis=0, tiled=True)  52.7 us
    all_to_all x1, waiting for transfers between devices, local(): parts = lax.all_to_all(send, 'req', split_axis=0, concat_axis=0, tiled=True)  45.9 us
    unnamed x42, local copies, waits for them, and re-layouts  13.3 us
    pallas_call x1, Pallas kernels, local(): pl.pallas_call(local_kernel, grid=(STEPS,), out_shape=(jax.ShapeDtypeStru...  11.6 us
    all_to_all x1, starting transfers between devices, local(): parts = lax.all_to_all(send, 'req', split_axis=0, concat_axis=0, tiled=True)  8.79 us
    unnamed x1, blocking collectives  7.88 us
    pallas_call x1, Pallas kernels, local(): pl.pallas_call(state_kernel, grid=(STEPS,), out_shape=(jax.ShapeDtypeStru...  7.04 us
  transfers between devices with their start and end apart: 2, of which 1 were waited for; matrix products, arithmetic and copies ran while one was open for 3% of the time, Pallas kernels for 5%

profile of v1, /device:TPU:13, one launch (start us, length us, event | category | flops | bytes accessed | tf_op | source)
XLA Modules:
  0.0 235.0 jit_solution(3448781793478379223)
XLA Ops:
  1.3 1.2 dynamic-slice
  2.6 0.8 dynamic-update-slice
  3.3 7.9 %all-reduce.1 = s32[16]{0:T(128)S(1)} all-reduce(s32[16]{0:T(128)S(1)} %dynamic-update-slice), channel_id=1, replica_groups=mesh['grp'=2,'req'=16] {'req'}, use_global_device_ids=true, to_apply=%add.1 | all-reduce | flops 16 | bytes 128
  11.2 1.3 compare_select_fusion.1
  14.5 3.1 %dynamic-slice_bitcast_fusion = bf16[16,8,8192]{2,1,0:T(8,128)(2,1)} fusion(bf16[3,128,8192]{2,1,0:T(8,128)(2,1)} %param.20, s32[]{:T(128)S(6)} %select_n.39), kind=kLoop, calls=%fused_computation.1 | loop fusion | bytes 4194308 | tf_op jit(solution)/shard_map/reshape | solution.py:115
  17.6 8.8 %all-to-all-start = ((bf16[16,8,8192]{2,1,0:T(8,128)(2,1)}), bf16[16,8,8192]{2,1,0:T(8,128)(2,1)S(1)}, u32[]{:S(2)}, u32[]{:S(2)}) async-start(bf16[16,8,8192]{2,1,0:T(8,128)(2,1)} %dynamic-slice_bitcast_fusion), calls=%async_computation | async-start | bytes 4194304 | tf_op jit(solution)/shard_map/all_to_all | solution.py:116
  26.4 1.2 gather_fusion
  27.6 0.1 copy.20
  27.8 0.1 compare_select_fusion
  27.9 45.9 %all-to-all-done.parts_ref = bf16[16,8,8192]{2,1,0:T(8,128)(2,1)S(1)} async-done(((bf16[16,8,8192]{2,1,0:T(8,128)(2,1)}), bf16[16,8,8192]{2,1,0:T(8,128)(2,1)S(1)}, u32[]{:S(2)}, u32[]{:S(2)}) %all-to-all-start) | async-done | bytes 2097184 | tf_op jit(solution)/shard_map/all_to_all | solution.py:116
  73.8 1.3 copy-done.13
  75.1 65.4 %pick.1 = bf16[16,8,8192]{2,1,0:T(8,128)(2,1)} custom-call(s32[16]{0:T(128)} %gather_fusion, bf16[16,8,8192]{2,1,0:T(8,128)(2,1)} %copy-done.13), custom_call_target="tpu_custom_call" | custom-call | tf_op jit(solution)/shard_map/pick/pallas_call | solution.py:32
  140.6 4.9 %all-to-all-start.1 = ((bf16[16,8,8192]{2,1,0:T(8,128)(2,1)}), bf16[16,8,8192]{2,1,0:T(8,128)(2,1)}, u32[]{:S(2)}, u32[]{:S(2)}) async-start(bf16[16,8,8192]{2,1,0:T(8,128)(2,1)} %pick.1), calls=%async_computation.1 | async-start | bytes 4194304 | tf_op jit(solution)/shard_map/all_to_all | solution.py:122
  145.5 0.3 fusion
  145.8 0.6 dynamic_slice.19
  147.7 0.6 dynamic_slice.16
  148.9 0.2 slice_reduce_fusion
  149.2 0.7 broadcast_in_dim_reshape.7.elast_ref
  150.0 0.7 broadcast_in_dim_reshape.6.skip_ref
  150.7 0.1 fusion.9
  150.8 1.0 copy.22
  151.8 0.2 copy.23
  152.0 1.0 copy.21
  153.7 52.7 %all_gather.7 = bf16[16,3,9216]{2,1,0:T(4,128)(2,1)S(1)} all-gather(bf16[1,3,9216]{2,1,0:T(4,128)(2,1)S(1)} %constant_dynamic-slice_fusion), channel_id=1, replica_groups=mesh['grp'=2,'req'=16] {'req'}, dimensions={0}, use_global_device_ids=true | all-gather | bytes 940032 | tf_op jit(solution)/shard_map/all_gather | solution.py:119
  206.6 0.7 copy-done.11
  207.3 11.6 %local.1 = (f32[128,8192]{1,0:T(8,128)S(1)}, f32[128,8192]{1,0:T(8,128)S(1)}, bf16[128,512]{1,0:T(8,128)(2,1)S(1)}) custom-call(bf16[128,9216]{1,0:T(8,128)(2,1)S(1)} %copy-done.1, bf16[128,9216]{1,0:T(8,128)(2,1)S(1)} %copy-done.1, bf16[128,9216]{1,0:T(8,128)(2,1)S(1)} %copy-done.1, f32[8,9216]{1,0:T(8,128)S(1)} %pad_convert_fusion.tx_ref.tb_ref.tc_ref, ...), custom_call_target="tpu_custom_call" | custom-call | flops 1000000000 | bytes 40000000 | tf_op jit(solution)/shard_map/local/pallas_call | solution.py:149
  218.9 2.0 copy-done.2
  220.9 2.0 copy-done.4
  222.9 2.2 copy-done.3
  225.1 2.2 copy-done.5
  227.2 0.8 copy-done.10
  228.0 7.0 %state.1 = (bf16[128,8192]{1,0:T(8,128)(2,1)}, bf16[1,128,8192]{2,1,0:T(8,128)(2,1)}) custom-call(s32[1]{0:T(128)S(6)} %convert_element_type.10.live_ref, bf16[128,8192]{1,0:T(8,128)(2,1)} %bitcast.3.start_ref, f32[128,8192]{1,0:T(8,128)S(1)} %copy-done.3, f32[128,8192]{1,0:T(8,128)S(1)} %copy-done.5, bf16[128,512]{1,0:T(8,128)(2,1)S(1)} %get-tuple-element.7.c_ref, ...), custom_call_target="tpu_custom_call" | custom-call | tf_op jit(solution)/shard_map/state/pallas_call | solution.py:166
  (41 shorter events, 0.4 us)
Async XLA Ops:
  0.6 153.0 %copy-start = (bf16[3,3,9216]{2,1,0:T(4,128)(2,1)S(1)}, bf16[3,3,9216]{2,1,0:T(4,128)(2,1)}, u32[]{:S(2)}) copy-start(bf16[3,3,9216]{2,1,0:T(4,128)(2,1)} %param.21) | copy-start | bytes 497668
  17.6 8.8 %copy-start.12 = (s32[16]{0:T(128)S(1)}, s32[16]{0:T(128)}, u32[]{:S(2)}) copy-start(s32[16]{0:T(128)} %param.22) | copy-start | bytes 196
  17.6 10.1 %copy-start.14 = (f32[128,128]{1,0:T(8,128)S(1)}, f32[128,128]{1,0:T(8,128)}, u32[]{:S(2)}) copy-start(f32[128,128]{1,0:T(8,128)} %param.14) | copy-start | bytes 196612
  17.6 10.2 %copy-start.17 = (f32[128]{0:T(128)S(1)}, f32[128]{0:T(128)}, u32[]{:S(2)}) copy-start(f32[128]{0:T(128)} %param.18) | copy-start | bytes 1540
  17.6 10.2 %copy-start.15 = (f32[128]{0:T(128)S(1)}, f32[128]{0:T(128)}, u32[]{:S(2)}) copy-start(f32[128]{0:T(128)} %param.17) | copy-start | bytes 1540
  17.6 56.2 %all-to-all-start = ((bf16[16,8,8192]{2,1,0:T(8,128)(2,1)}), bf16[16,8,8192]{2,1,0:T(8,128)(2,1)S(1)}, u32[]{:S(2)}, u32[]{:S(2)}) async-start(bf16[16,8,8192]{2,1,0:T(8,128)(2,1)} %dynamic-slice_bitcast_fusion), calls=%async_computation | async-start | bytes 4194304 | tf_op jit(solution)/shard_map/all_to_all | solution.py:116
  73.8 1.3 copy-start.13
  140.6 7.1 %copy-start.18 = (s32[16]{0:T(128)S(1)}, s32[16]{0:T(128)}, u32[]{:S(2)}) copy-start(s32[16]{0:T(128)} %param.24) | copy-start | bytes 196
  140.6 9.3 %copy-start.16 = (f32[128]{0:T(128)S(1)}, f32[128]{0:T(128)}, u32[]{:S(2)}) copy-start(f32[128]{0:T(128)} %param.19) | copy-start | bytes 1540
  140.6 82.3 %all-to-all-start.1 = ((bf16[16,8,8192]{2,1,0:T(8,128)(2,1)}), bf16[16,8,8192]{2,1,0:T(8,128)(2,1)}, u32[]{:S(2)}, u32[]{:S(2)}) async-start(bf16[16,8,8192]{2,1,0:T(8,128)(2,1)} %pick.1), calls=%async_computation.1 | async-start | bytes 4194304 | tf_op jit(solution)/shard_map/all_to_all | solution.py:122
  149.2 57.3 %copy-start.1 = (bf16[128,9216]{1,0:T(8,128)(2,1)S(1)}, bf16[128,9216]{1,0:T(8,128)(2,1)}, u32[]{:S(2)}) copy-start(bf16[128,9216]{1,0:T(8,128)(2,1)} %xc_ref.1) | copy-start | bytes 7077892
  149.2 57.3 %copy-start.8 = (f32[4,9216]{1,0:T(4,128)S(1)}, f32[4,9216]{1,0:T(4,128)}, u32[]{:S(2)}) copy-start(f32[4,9216]{1,0:T(4,128)} %wc_ref.1) | copy-start | bytes 442372
  149.2 57.3 %copy-start.9 = (f32[9216]{0:T(1024)S(1)}, f32[9216]{0:T(1024)}, u32[]{:S(2)}) copy-start(f32[9216]{0:T(1024)} %param.16) | copy-start | bytes 110596
  153.7 52.9 %copy-start.6 = (f32[128,8,16]{2,0,1:T(8,128)S(1)}, f32[128,8,16]{2,0,1:T(8,128)}, u32[]{:S(2)}) copy-start(f32[128,8,16]{2,0,1:T(8,128)} %copy.22) | copy-start | bytes 196612
  153.7 52.9 %copy-start.7 = (f32[128,8,16]{2,0,1:T(8,128)S(1)}, f32[128,8,16]{2,0,1:T(8,128)}, u32[]{:S(2)}) copy-start(f32[128,8,16]{2,0,1:T(8,128)} %copy.21) | copy-start | bytes 196612
  206.6 0.8 copy-start.11
  218.9 2.0 copy-start.2
  220.9 2.0 copy-start.4
  222.9 2.2 copy-start.3
  225.0 2.2 copy-start.5
  227.2 0.8 copy-start.10

commit v2 on v1

--- a/solution.py
+++ b/solution.py
@@ -32,7 +32,7 @@
     return pl.pallas_call(
         pick_kernel,
         out_shape=jax.ShapeDtypeStruct((count,) + parts.shape[1:], parts.dtype),
-        in_specs=[pl.BlockSpec(memory_space=pltpu.SMEM), pl.BlockSpec(memory_space=pl.ANY)],
+        in_specs=[pl.BlockSpec(memory_space=pltpu.SMEM), pl.BlockSpec(memory_space=pltpu.VMEM)],
         out_specs=pl.BlockSpec(memory_space=pl.ANY),
         scratch_shapes=[pltpu.SemaphoreType.DMA((count,))],
         name="pick",
@@ -113,11 +113,13 @@
     device = lax.axis_index("req")
     served = jnp.max(jnp.where(hit_owner == device, hit_slot, 0))
     send = lax.dynamic_slice_in_dim(cache_states, served, 1, 0).reshape(count, NST // count, INNER)
+    own_tail = lax.dynamic_slice_in_dim(cache_tails, served, 1, 0)
+    own_request = jnp.full((1, 1, own_tail.shape[2]), mine.astype(own_tail.dtype))
+    gathered = lax.all_gather(jnp.concatenate([own_tail, own_request], axis=1), "req", axis=0, tiled=True)
+    send, gathered = lax.optimization_barrier((send, gathered))
+    every_tail, every_request = gathered[:, :3], gathered[:, 3, 0].astype(jnp.int32)
     parts = lax.all_to_all(send, "req", split_axis=0, concat_axis=0, tiled=True)
 
-    own_tail = lax.dynamic_slice_in_dim(cache_tails, served, 1, 0)
-    every_tail = lax.all_gather(own_tail, "req", axis=0, tiled=True)
-    every_request = lax.all_gather(request_of, "req", axis=0, tiled=True)
     chosen = pick(parts, hit_owner[every_request])
     start = lax.all_to_all(chosen, "req", split_axis=0, concat_axis=0, tiled=True).reshape(NST, INNER)
 
@@ -157,7 +159,7 @@
         in_specs=triple(rows) + triple(8) + triple(4) + triple(1) + [tall, flat, flat, tall, wide(1)],
         out_specs=(wide(rows), wide(NST), group),
         scratch_shapes=[pltpu.VMEM((8 + rows, COLS), jnp.float32)],
-        compiler_params=pltpu.CompilerParams(vmem_limit_bytes=40 * 2**20),
+        compiler_params=pltpu.CompilerParams(vmem_limit_bytes=58 * 2**20),
         cost_estimate=pl.CostEstimate(flops=10**9, bytes_accessed=40 * 10**6, transcendentals=4 * 10**6),
         name="local",
     )(xbc, xbc, xbc, tail, tail, tail, conv_weight, conv_weight, conv_weight, bias, bias, bias,
@@ -172,7 +174,7 @@
         ),
         in_specs=[pl.BlockSpec(memory_space=pltpu.SMEM), wide(NST), wide(rows), wide(NST), group, tall, wide(1)],
         out_specs=(wide(rows), pl.BlockSpec((1, NST, COLS), lambda i: (0, 0, i))),
-        compiler_params=pltpu.CompilerParams(vmem_limit_bytes=40 * 2**20),
+        compiler_params=pltpu.CompilerParams(vmem_limit_bytes=58 * 2**20),
         name="state",
     )(live[None], start, y_local, fresh, c_part, by_step(jnp.exp(cum)), elast)
 

time: 237 us -> 178 us (0.75)
  blocking collectives: 60.5 us -> 0 us
  Pallas kernels: 84.1 us -> 25.2 us
  waiting for transfers between devices: 45.9 us -> 104 us
  between operations: 6.12 us -> 19.4 us
  local copies, waits for them, and re-layouts: 22.8 us -> 13.8 us
  starting transfers between devices: 13.7 us -> 10.5 us
  other arithmetic: 1.63 us -> 4.36 us
    pallas_call x1, Pallas kernels: 65.4 us -> 3.04 us  [pick(): pl.pallas_call(pick_kernel, out_shape=jax.ShapeDtypeStruct((count,) + par...]
    all_gather x1 -> x0, blocking collectives: 52.7 us -> none  [local(): every_tail = lax.all_gather(own_tail, 'req', axis=0, tiled=True)]
    all_gather x0 -> x1, waiting for transfers between devices: none -> 35.5 us  [local(): lax.all_gather(jnp.concatenate([own_tail, own_request], axis=1), 'req', a...]
    all_to_all x1, waiting for transfers between devices: 0.01 us -> 23.2 us  [local(): lax.all_to_all(chosen, 'req', split_axis=0, concat_axis=0, tiled=True)]
    unnamed x42 -> x23, local copies, waits for them, and re-layouts: 13.3 us -> 2.83 us
    unnamed x1 -> x0, blocking collectives: 7.88 us -> none
    all_to_all x1, starting transfers between devices: 8.79 us -> 5.45 us  [local(): parts = lax.all_to_all(send, 'req', split_axis=0, concat_axis=0, tiled=True)]
  transfers between devices with their start and end apart: 2 -> 3, of which waited for: 1 -> 3; matrix products, arithmetic and copies ran while one was open for 3% -> 8% of each run, Pallas kernels for 5% -> 7%
where the time goes in v2:
time: 178 us; the launch traced here: 177 us
  waiting for transfers between devices  104 us (58%)
  Pallas kernels  25.2 us (14%)
  between operations  19.4 us (11%)
  local copies, waits for them, and re-layouts  13.8 us (8%)
  starting transfers between devices  10.5 us (6%)
  other arithmetic  4.36 us (2%)
    all_to_all x1, waiting for transfers between devices, local(): parts = lax.all_to_all(send, 'req', split_axis=0, concat_axis=0, tiled=True)  45 us
    all_gather x1, waiting for transfers between devices, local(): lax.all_gather(jnp.concatenate([own_tail, own_request], axis=1), 'req', a...  35.5 us
    all_to_all x1, waiting for transfers between devices, local(): lax.all_to_all(chosen, 'req', split_axis=0, concat_axis=0, tiled=True)  23.2 us
    pallas_call x1, Pallas kernels, local(): pl.pallas_call(local_kernel, grid=(STEPS,), out_shape=(jax.ShapeDtypeStru...  13.3 us
    pallas_call x1, Pallas kernels, local(): pl.pallas_call(state_kernel, grid=(STEPS,), out_shape=(jax.ShapeDtypeStru...  8.86 us
    all_to_all x1, starting transfers between devices, local(): parts = lax.all_to_all(send, 'req', split_axis=0, concat_axis=0, tiled=True)  5.45 us
    all_to_all x1, starting transfers between devices, local(): lax.all_to_all(chosen, 'req', split_axis=0, concat_axis=0, tiled=True)  5.05 us
  transfers between devices with their start and end apart: 3, of which 3 were waited for; matrix products, arithmetic and copies ran while one was open for 8% of the time, Pallas kernels for 7%

profile of v2, /device:TPU:13, one launch (start us, length us, event | category | flops | bytes accessed | tf_op | source)
XLA Modules:
  0.0 177.4 jit_solution(17385620315604318153)
XLA Ops:
  7.2 0.0 all-gather.2.cloned.1.call-start
  7.9 1.3 fusion.6
  11.2 0.7 concatenate.3
  11.9 3.1 %dynamic-slice_bitcast_fusion = bf16[16,8,8192]{2,1,0:T(8,128)(2,1)} fusion(bf16[3,128,8192]{2,1,0:T(8,128)(2,1)} %param.20, s32[]{:T(128)S(6)} %select_n.45), kind=kLoop, calls=%fused_computation.1 | loop fusion | bytes 4194308 | tf_op jit(solution)/shard_map/reshape | solution.py:115
  15.0 35.5 %all-gather.2.cloned.1.call-done = bf16[16,4,9216]{2,1,0:T(4,128)(2,1)} async-done(((bf16[1,4,9216]{2,1,0:T(4,128)(2,1)}), bf16[16,4,9216]{2,1,0:T(4,128)(2,1)}) %all-gather.2.cloned.1.call-update) | async-done | bytes 1179664 | tf_op jit(solution)/shard_map/all_gather | solution.py:118
  50.5 5.4 %all-to-all-start = ((bf16[16,8,8192]{2,1,0:T(8,128)(2,1)}), bf16[16,8,8192]{2,1,0:T(8,128)(2,1)S(1)}, u32[]{:S(2)}, u32[]{:S(2)}) async-start(bf16[16,8,8192]{2,1,0:T(8,128)(2,1)} %dynamic-slice_bitcast_fusion), calls=%async_computation | async-start | bytes 4194304 | tf_op jit(solution)/shard_map/all_to_all | solution.py:121
  56.0 1.1 convert_reduce_fusion
  57.1 1.2 gather_fusion
  58.4 45.0 %all-to-all-done.parts_ref = bf16[16,8,8192]{2,1,0:T(8,128)(2,1)S(1)} async-done(((bf16[16,8,8192]{2,1,0:T(8,128)(2,1)}), bf16[16,8,8192]{2,1,0:T(8,128)(2,1)S(1)}, u32[]{:S(2)}, u32[]{:S(2)}) %all-to-all-start) | async-done | bytes 2097184 | tf_op jit(solution)/shard_map/all_to_all | solution.py:121
  103.4 1.3 copy-done.2
  104.7 3.0 %pick.1 = bf16[16,8,8192]{2,1,0:T(8,128)(2,1)} custom-call(s32[16]{0:T(128)} %gather_fusion, bf16[16,8,8192]{2,1,0:T(8,128)(2,1)} %copy-done.2), custom_call_target="tpu_custom_call" | custom-call | tf_op jit(solution)/shard_map/pick/pallas_call | solution.py:32
  107.8 5.1 %all-to-all-start.1 = ((bf16[16,8,8192]{2,1,0:T(8,128)(2,1)}), bf16[16,8,8192]{2,1,0:T(8,128)(2,1)S(1)}, u32[]{:S(2)}, u32[]{:S(2)}) async-start(bf16[16,8,8192]{2,1,0:T(8,128)(2,1)} %pick.1), calls=%async_computation.1 | async-start | bytes 4194304 | tf_op jit(solution)/shard_map/all_to_all | solution.py:124
  112.9 0.6 dynamic_slice.19
  114.7 0.6 dynamic_slice.16
  116.0 0.1 copy.20
  116.1 0.1 compare_select_fusion
  116.2 0.3 fusion
  116.5 0.2 slice_reduce_fusion
  116.7 0.1 broadcast_in_dim.37
  116.8 0.7 broadcast_in_dim_reshape.7.elast_ref
  117.5 0.1 broadcast_in_dim.36
  117.6 0.7 broadcast_in_dim_reshape.6.skip_ref
  118.3 0.1 fusion.10
  118.4 1.0 copy.22
  119.4 1.0 copy.23
  120.5 1.0 copy.21
  122.1 0.9 select_bitcast_fusion
  123.0 0.8 pad_convert_fusion.tx_ref.tb_ref.tc_ref
  123.8 13.3 %local.1 = (f32[128,8192]{1,0:T(8,128)}, f32[128,8192]{1,0:T(8,128)}, bf16[128,512]{1,0:T(8,128)(2,1)}) custom-call(bf16[128,9216]{1,0:T(8,128)(2,1)} %xc_ref.1, bf16[128,9216]{1,0:T(8,128)(2,1)} %xc_ref.1, bf16[128,9216]{1,0:T(8,128)(2,1)} %xc_ref.1, f32[8,9216]{1,0:T(8,128)} %pad_convert_fusion.tx_ref.tb_ref.tc_ref, ...), custom_call_target="tpu_custom_call" | custom-call | flops 1000000000 | bytes 40000000 | tf_op jit(solution)/shard_map/local/pallas_call | solution.py:151
  137.1 23.2 %all-to-all-done.1 = bf16[16,8,8192]{2,1,0:T(8,128)(2,1)S(1)} async-done(((bf16[16,8,8192]{2,1,0:T(8,128)(2,1)}), bf16[16,8,8192]{2,1,0:T(8,128)(2,1)S(1)}, u32[]{:S(2)}, u32[]{:S(2)}) %all-to-all-start.1) | async-done | bytes 2097184 | tf_op jit(solution)/shard_map/all_to_all | solution.py:124
  160.3 1.4 copy-done.3
  161.7 8.9 %state.1 = (bf16[128,8192]{1,0:T(8,128)(2,1)}, bf16[1,128,8192]{2,1,0:T(8,128)(2,1)}) custom-call(s32[1]{0:T(128)S(6)} %convert_element_type.26.live_ref, bf16[128,8192]{1,0:T(8,128)(2,1)} %bitcast.30, f32[128,8192]{1,0:T(8,128)} %get-tuple-element.9.y_ref, f32[128,8192]{1,0:T(8,128)} %get-tuple-element.10.fresh_ref, ...), custom_call_target="tpu_custom_call" | custom-call | tf_op jit(solution)/shard_map/state/pallas_call | solution.py:168
  (26 shorter events, 0.1 us)
Async XLA Ops:
  7.2 4.0 %copy-start = (bf16[3,3,9216]{2,1,0:T(4,128)(2,1)S(1)}, bf16[3,3,9216]{2,1,0:T(4,128)(2,1)}, u32[]{:S(2)}) copy-start(bf16[3,3,9216]{2,1,0:T(4,128)(2,1)} %param.21) | copy-start | bytes 497668
  7.2 43.4 %all-gather.2.cloned.1.call-start = ((), (), s32[]{:S(2)}) async-start(), calls=%async_computation.2 | async-start | bytes 1253376 | tf_op jit(solution)/shard_map/all_gather | solution.py:118
  15.0 42.1 %copy-start.1 = (s32[16]{0:T(128)S(1)}, s32[16]{0:T(128)}, u32[]{:S(2)}) copy-start(s32[16]{0:T(128)} %param.22) | copy-start | bytes 196
  50.5 52.9 %all-to-all-start = ((bf16[16,8,8192]{2,1,0:T(8,128)(2,1)}), bf16[16,8,8192]{2,1,0:T(8,128)(2,1)S(1)}, u32[]{:S(2)}, u32[]{:S(2)}) async-start(bf16[16,8,8192]{2,1,0:T(8,128)(2,1)} %dynamic-slice_bitcast_fusion), calls=%async_computation | async-start | bytes 4194304 | tf_op jit(solution)/shard_map/all_to_all | solution.py:121
  103.4 1.3 copy-start.2
  107.8 7.0 %copy-start.9 = (s32[16]{0:T(128)S(1)}, s32[16]{0:T(128)}, u32[]{:S(2)}) copy-start(s32[16]{0:T(128)} %param.24) | copy-start | bytes 196
  107.8 8.2 %copy-start.6 = (f32[128,128]{1,0:T(8,128)S(1)}, f32[128,128]{1,0:T(8,128)}, u32[]{:S(2)}) copy-start(f32[128,128]{1,0:T(8,128)} %param.14) | copy-start | bytes 196612
  107.8 8.3 %copy-start.10 = (f32[128]{0:T(128)S(1)}, f32[128]{0:T(128)}, u32[]{:S(2)}) copy-start(f32[128]{0:T(128)} %param.18) | copy-start | bytes 1540
  107.8 8.3 %copy-start.7 = (f32[128]{0:T(128)S(1)}, f32[128]{0:T(128)}, u32[]{:S(2)}) copy-start(f32[128]{0:T(128)} %param.17) | copy-start | bytes 1540
  107.8 9.7 %copy-start.8 = (f32[128]{0:T(128)S(1)}, f32[128]{0:T(128)}, u32[]{:S(2)}) copy-start(f32[128]{0:T(128)} %param.19) | copy-start | bytes 1540
  107.8 52.5 %all-to-all-start.1 = ((bf16[16,8,8192]{2,1,0:T(8,128)(2,1)}), bf16[16,8,8192]{2,1,0:T(8,128)(2,1)S(1)}, u32[]{:S(2)}, u32[]{:S(2)}) async-start(bf16[16,8,8192]{2,1,0:T(8,128)(2,1)} %pick.1), calls=%async_computation.1 | async-start | bytes 4194304 | tf_op jit(solution)/shard_map/all_to_all | solution.py:124
  116.2 7.6 %copy-start.5 = (f32[128,128]{0,1:T(8,128)}, f32[128,128]{0,1:T(8,128)S(1)}, u32[]{:S(2)}) copy-start(f32[128,128]{0,1:T(8,128)S(1)} %compare_select_fusion) | copy-start | bytes 196612
  116.5 7.3 %copy-start.4 = (f32[128,128]{0,1:T(8,128)}, f32[128,128]{0,1:T(8,128)S(1)}, u32[]{:S(2)}) copy-start(f32[128,128]{0,1:T(8,128)S(1)} %fusion) | copy-start | bytes 196612
  160.3 1.4 copy-start.3
Sparse Core Ops, SparseCore 0:
  12.1 38.4 all-gather.1

commit v3 on v2

--- a/solution.py
+++ b/solution.py
@@ -116,7 +116,6 @@
     own_tail = lax.dynamic_slice_in_dim(cache_tails, served, 1, 0)
     own_request = jnp.full((1, 1, own_tail.shape[2]), mine.astype(own_tail.dtype))
     gathered = lax.all_gather(jnp.concatenate([own_tail, own_request], axis=1), "req", axis=0, tiled=True)
-    send, gathered = lax.optimization_barrier((send, gathered))
     every_tail, every_request = gathered[:, :3], gathered[:, 3, 0].astype(jnp.int32)
     parts = lax.all_to_all(send, "req", split_axis=0, concat_axis=0, tiled=True)
 

time: 178 us -> 155 us (0.87)
  waiting for transfers between devices: 104 us -> 78.9 us
  starting transfers between devices: 10.5 us -> 12.6 us
    all_to_all x1, waiting for transfers between devices: 45 us -> 0.01 us  [local(): parts = lax.all_to_all(send, 'req', split_axis=0, concat_axis=0, tiled=True)]
    all_gather x1, waiting for transfers between devices: 35.5 us -> 55.6 us  [local(): lax.all_gather(jnp.concatenate([own_tail, own_request], axis=1), 'req', a...]
  transfers between devices with their start and end apart: 3 -> 3, of which waited for: 3 -> 2; matrix products, arithmetic and copies ran while one was open for 8% -> 7% of each run, Pallas kernels for 7% -> 9%
where the time goes in v3:
time: 155 us
  waiting for transfers between devices  78.9 us (51%)
  Pallas kernels  25.1 us (16%)
  between operations  19.4 us (13%)
  local copies, waits for them, and re-layouts  13.8 us (9%)
  starting transfers between devices  12.6 us (8%)
  other arithmetic  4.4 us (3%)
    all_gather x1, waiting for transfers between devices, local(): lax.all_gather(jnp.concatenate([own_tail, own_request], axis=1), 'req', a...  55.6 us
    all_to_all x1, waiting for transfers between devices, local(): lax.all_to_all(chosen, 'req', split_axis=0, concat_axis=0, tiled=True)  23.3 us
    pallas_call x1, Pallas kernels, local(): pl.pallas_call(local_kernel, grid=(STEPS,), out_shape=(jax.ShapeDtypeStru...  13.3 us
    pallas_call x1, Pallas kernels, local(): pl.pallas_call(state_kernel, grid=(STEPS,), out_shape=(jax.ShapeDtypeStru...  8.85 us
    all_to_all x1, starting transfers between devices, local(): parts = lax.all_to_all(send, 'req', split_axis=0, concat_axis=0, tiled=True)  6.69 us
    all_to_all x1, starting transfers between devices, local(): lax.all_to_all(chosen, 'req', split_axis=0, concat_axis=0, tiled=True)  5.89 us
  transfers between devices with their start and end apart: 3, of which 2 were waited for; matrix products, arithmetic and copies ran while one was open for 7% of the time, Pallas kernels for 9%

profile of v3, /device:TPU:13, one launch (start us, length us, event | category | flops | bytes accessed | tf_op | source)
XLA Modules:
  0.0 154.6 jit_solution(8069146382513320924)
XLA Ops:
  7.2 1.3 fusion.7
  10.5 3.1 %dynamic-slice_bitcast_fusion = bf16[16,8,8192]{2,1,0:T(8,128)(2,1)} fusion(bf16[3,128,8192]{2,1,0:T(8,128)(2,1)} %param.20, s32[]{:T(128)S(6)} %select_n.45), kind=kLoop, calls=%fused_computation.1 | loop fusion | bytes 4194308 | tf_op jit(solution)/shard_map/reshape | solution.py:115
  13.6 6.7 %all-to-all-start = ((bf16[16,8,8192]{2,1,0:T(8,128)(2,1)}), bf16[16,8,8192]{2,1,0:T(8,128)(2,1)S(1)}, u32[]{:S(2)}, u32[]{:S(2)}) async-start(bf16[16,8,8192]{2,1,0:T(8,128)(2,1)} %dynamic-slice_bitcast_fusion), calls=%async_computation | async-start | bytes 4194304 | tf_op jit(solution)/shard_map/all_to_all | solution.py:120
  20.3 0.0 all-gather.2.cloned.1.call-start
  21.0 0.7 concatenate.3
  21.7 0.0 all-gather.2.cloned.1.call-update
  21.7 55.6 %all-gather.2.cloned.1.call-done = bf16[16,4,9216]{2,1,0:T(4,128)(2,1)} async-done(((bf16[1,4,9216]{2,1,0:T(4,128)(2,1)}), bf16[16,4,9216]{2,1,0:T(4,128)(2,1)}) %all-gather.2.cloned.1.call-update) | async-done | bytes 1179664 | tf_op jit(solution)/shard_map/all_gather | solution.py:118
  77.4 1.1 fusion.6
  78.5 1.2 gather_fusion
  79.7 1.3 copy-done.2
  81.1 3.0 %pick.1 = bf16[16,8,8192]{2,1,0:T(8,128)(2,1)} custom-call(s32[16]{0:T(128)} %gather_fusion, bf16[16,8,8192]{2,1,0:T(8,128)(2,1)} %copy-done.2), custom_call_target="tpu_custom_call" | custom-call | tf_op jit(solution)/shard_map/pick/pallas_call | solution.py:32
  84.2 5.9 %all-to-all-start.1 = ((bf16[16,8,8192]{2,1,0:T(8,128)(2,1)}), bf16[16,8,8192]{2,1,0:T(8,128)(2,1)S(1)}, u32[]{:S(2)}, u32[]{:S(2)}) async-start(bf16[16,8,8192]{2,1,0:T(8,128)(2,1)} %pick.1), calls=%async_computation.1 | async-start | bytes 4194304 | tf_op jit(solution)/shard_map/all_to_all | solution.py:123
  90.1 0.6 dynamic_slice.19
  91.9 0.6 dynamic_slice.16
  93.2 0.1 copy.20
  93.3 0.1 compare_select_fusion
  93.4 0.3 fusion
  93.7 0.2 slice_reduce_fusion
  93.9 0.1 broadcast_in_dim.37
  94.0 0.7 broadcast_in_dim_reshape.7.elast_ref
  94.7 0.1 broadcast_in_dim.36
  94.8 0.7 broadcast_in_dim_reshape.6.skip_ref
  95.5 0.1 fusion.11
  95.6 1.0 copy.22
  96.6 1.0 copy.23
  97.6 1.0 copy.21
  99.3 0.9 select_bitcast_fusion
  100.2 0.8 pad_convert_fusion.tx_ref.tb_ref.tc_ref
  101.0 13.3 %local.1 = (f32[128,8192]{1,0:T(8,128)}, f32[128,8192]{1,0:T(8,128)}, bf16[128,512]{1,0:T(8,128)(2,1)}) custom-call(bf16[128,9216]{1,0:T(8,128)(2,1)} %xc_ref.1, bf16[128,9216]{1,0:T(8,128)(2,1)} %xc_ref.1, bf16[128,9216]{1,0:T(8,128)(2,1)} %xc_ref.1, f32[8,9216]{1,0:T(8,128)} %pad_convert_fusion.tx_ref.tb_ref.tc_ref, ...), custom_call_target="tpu_custom_call" | custom-call | flops 1000000000 | bytes 40000000 | tf_op jit(solution)/shard_map/local/pallas_call | solution.py:150
  114.2 23.3 %all-to-all-done.1 = bf16[16,8,8192]{2,1,0:T(8,128)(2,1)S(1)} async-done(((bf16[16,8,8192]{2,1,0:T(8,128)(2,1)}), bf16[16,8,8192]{2,1,0:T(8,128)(2,1)S(1)}, u32[]{:S(2)}, u32[]{:S(2)}) %all-to-all-start.1) | async-done | bytes 2097184 | tf_op jit(solution)/shard_map/all_to_all | solution.py:123
  137.5 1.4 copy-done.3
  138.9 8.9 %state.1 = (bf16[128,8192]{1,0:T(8,128)(2,1)}, bf16[1,128,8192]{2,1,0:T(8,128)(2,1)}) custom-call(s32[1]{0:T(128)S(6)} %convert_element_type.26.live_ref, bf16[128,8192]{1,0:T(8,128)(2,1)} %bitcast.30, f32[128,8192]{1,0:T(8,128)} %get-tuple-element.5.y_ref, f32[128,8192]{1,0:T(8,128)} %get-tuple-element.6.fresh_ref, ...), custom_call_target="tpu_custom_call" | custom-call | tf_op jit(solution)/shard_map/state/pallas_call | solution.py:167
  (26 shorter events, 0.1 us)
Async XLA Ops:
  7.2 13.8 %copy-start = (bf16[3,3,9216]{2,1,0:T(4,128)(2,1)S(1)}, bf16[3,3,9216]{2,1,0:T(4,128)(2,1)}, u32[]{:S(2)}) copy-start(bf16[3,3,9216]{2,1,0:T(4,128)(2,1)} %param.21) | copy-start | bytes 497668
  13.6 64.9 %copy-start.1 = (s32[16]{0:T(128)S(1)}, s32[16]{0:T(128)}, u32[]{:S(2)}) copy-start(s32[16]{0:T(128)} %param.22) | copy-start | bytes 196
  13.6 66.2 %all-to-all-start = ((bf16[16,8,8192]{2,1,0:T(8,128)(2,1)}), bf16[16,8,8192]{2,1,0:T(8,128)(2,1)S(1)}, u32[]{:S(2)}, u32[]{:S(2)}) async-start(bf16[16,8,8192]{2,1,0:T(8,128)(2,1)} %dynamic-slice_bitcast_fusion), calls=%async_computation | async-start | bytes 4194304 | tf_op jit(solution)/shard_map/all_to_all | solution.py:120
  20.3 57.1 %all-gather.2.cloned.1.call-start = ((), (), s32[]{:S(2)}) async-start(), calls=%async_computation.2 | async-start | bytes 1253376 | tf_op jit(solution)/shard_map/all_gather | solution.py:118
  79.7 1.3 copy-start.2
  84.1 7.8 %copy-start.9 = (s32[16]{0:T(128)S(1)}, s32[16]{0:T(128)}, u32[]{:S(2)}) copy-start(s32[16]{0:T(128)} %param.24) | copy-start | bytes 196
  84.1 9.0 %copy-start.6 = (f32[128,128]{1,0:T(8,128)S(1)}, f32[128,128]{1,0:T(8,128)}, u32[]{:S(2)}) copy-start(f32[128,128]{1,0:T(8,128)} %param.14) | copy-start | bytes 196612
  84.1 9.1 %copy-start.10 = (f32[128]{0:T(128)S(1)}, f32[128]{0:T(128)}, u32[]{:S(2)}) copy-start(f32[128]{0:T(128)} %param.18) | copy-start | bytes 1540
  84.1 9.1 %copy-start.7 = (f32[128]{0:T(128)S(1)}, f32[128]{0:T(128)}, u32[]{:S(2)}) copy-start(f32[128]{0:T(128)} %param.17) | copy-start | bytes 1540
  84.1 10.5 %copy-start.8 = (f32[128]{0:T(128)S(1)}, f32[128]{0:T(128)}, u32[]{:S(2)}) copy-start(f32[128]{0:T(128)} %param.19) | copy-start | bytes 1540
  84.2 53.3 %all-to-all-start.1 = ((bf16[16,8,8192]{2,1,0:T(8,128)(2,1)}), bf16[16,8,8192]{2,1,0:T(8,128)(2,1)S(1)}, u32[]{:S(2)}, u32[]{:S(2)}) async-start(bf16[16,8,8192]{2,1,0:T(8,128)(2,1)} %pick.1), calls=%async_computation.1 | async-start | bytes 4194304 | tf_op jit(solution)/shard_map/all_to_all | solution.py:123
  93.4 7.6 %copy-start.5 = (f32[128,128]{0,1:T(8,128)}, f32[128,128]{0,1:T(8,128)S(1)}, u32[]{:S(2)}) copy-start(f32[128,128]{0,1:T(8,128)S(1)} %compare_select_fusion) | copy-start | bytes 196612
  93.7 7.3 %copy-start.4 = (f32[128,128]{0,1:T(8,128)}, f32[128,128]{0,1:T(8,128)S(1)}, u32[]{:S(2)}) copy-start(f32[128,128]{0,1:T(8,128)S(1)} %fusion) | copy-start | bytes 196612
  137.5 1.4 copy-start.3
Sparse Core Ops, SparseCore 0:
  24.0 53.3 all-gather.1

commit v4 on v3

--- a/solution.py
+++ b/solution.py
@@ -20,7 +20,7 @@
     count = out_ref.shape[0]
     copies = []
     for i in range(count):
-        copy = pltpu.make_async_copy(parts_ref.at[index_ref[i]], out_ref.at[i], sem.at[i])
+        copy = pltpu.make_async_copy(parts_ref.at[index_ref[i], :, pl.ds(0, INNER)], out_ref.at[i], sem.at[i])
         copy.start()
         copies.append(copy)
     for copy in copies:
@@ -31,10 +31,11 @@
     count = index.shape[0]
     return pl.pallas_call(
         pick_kernel,
-        out_shape=jax.ShapeDtypeStruct((count,) + parts.shape[1:], parts.dtype),
+        out_shape=jax.ShapeDtypeStruct((count, parts.shape[1], INNER), parts.dtype),
         in_specs=[pl.BlockSpec(memory_space=pltpu.SMEM), pl.BlockSpec(memory_space=pltpu.VMEM)],
         out_specs=pl.BlockSpec(memory_space=pl.ANY),
         scratch_shapes=[pltpu.SemaphoreType.DMA((count,))],
+        compiler_params=pltpu.CompilerParams(vmem_limit_bytes=8 * 2**20),
         name="pick",
     )(index, parts)
 
@@ -113,13 +114,18 @@
     device = lax.axis_index("req")
     served = jnp.max(jnp.where(hit_owner == device, hit_slot, 0))
     send = lax.dynamic_slice_in_dim(cache_states, served, 1, 0).reshape(count, NST // count, INNER)
+    number = jnp.broadcast_to(mine.astype(send.dtype), send.shape[:2] + (128,))
+    parts = lax.all_to_all(
+        jnp.concatenate([send, number], axis=2), "req", split_axis=0, concat_axis=0, tiled=True
+    )
+    every_request = parts[:, 0, INNER].astype(jnp.int32)
     own_tail = lax.dynamic_slice_in_dim(cache_tails, served, 1, 0)
-    own_request = jnp.full((1, 1, own_tail.shape[2]), mine.astype(own_tail.dtype))
-    gathered = lax.all_gather(jnp.concatenate([own_tail, own_request], axis=1), "req", axis=0, tiled=True)
-    every_tail, every_request = gathered[:, :3], gathered[:, 3, 0].astype(jnp.int32)
-    parts = lax.all_to_all(send, "req", split_axis=0, concat_axis=0, tiled=True)
-
-    chosen = pick(parts, hit_owner[every_request])
+    own_tail = jnp.pad(own_tail, ((0, 0), (0, 1), (0, 0)))
+    every_tail = lax.all_gather(own_tail, "req", axis=0, tiled=True)[:, :3]
+    owners = jnp.sum(
+        jnp.where(every_request[:, None] == jnp.arange(count)[None, :], hit_owner[None, :], 0), axis=1
+    )
+    chosen = pick(parts, owners)
     start = lax.all_to_all(chosen, "req", split_axis=0, concat_axis=0, tiled=True).reshape(NST, INNER)
 
     tail = lax.dynamic_index_in_dim(every_tail, hit_owner[mine], 0, keepdims=False)

time: 155 us -> 151 us (0.974)
  starting transfers between devices: 12.6 us -> 10.8 us
    all_gather x1, waiting for transfers between devices: 55.6 us -> 0.02 us  [local(): every_tail = lax.all_gather(own_tail, 'req', axis=0, tiled=True)[:, :3]]
    all_to_all x1, waiting for transfers between devices: 0.01 us -> 54.7 us  [local(): lax.all_to_all(jnp.concatenate([send, number], axis=2), 'req', split_axis...]
    all_to_all x1, starting transfers between devices: 5.89 us -> 4.11 us  [local(): lax.all_to_all(chosen, 'req', split_axis=0, concat_axis=0, tiled=True)]
  transfers between devices with their start and end apart: 3 -> 3, of which waited for: 2 -> 2; matrix products, arithmetic and copies ran while one was open for 7% -> 6% of each run, Pallas kernels for 9% -> 11%
where the time goes in v4:
time: 151 us
  waiting for transfers between devices  78.1 us (52%)
  Pallas kernels  25.7 us (17%)
  between operations  19.2 us (13%)
  local copies, waits for them, and re-layouts  12.8 us (8%)
  starting transfers between devices  10.8 us (7%)
  other arithmetic  3.81 us (3%)
    all_to_all x1, waiting for transfers between devices, local(): lax.all_to_all(jnp.concatenate([send, number], axis=2), 'req', split_axis...  54.7 us
    all_to_all x1, waiting for transfers between devices, local(): lax.all_to_all(chosen, 'req', split_axis=0, concat_axis=0, tiled=True)  23.3 us
    pallas_call x1, Pallas kernels, local(): pl.pallas_call(local_kernel, grid=(STEPS,), out_shape=(jax.ShapeDtypeStru...  13.3 us
    pallas_call x1, Pallas kernels, local(): pl.pallas_call(state_kernel, grid=(STEPS,), out_shape=(jax.ShapeDtypeStru...  8.85 us
    all_to_all x1, starting transfers between devices, local(): lax.all_to_all(jnp.concatenate([send, number], axis=2), 'req', split_axis...  6.69 us
    all_to_all x1, starting transfers between devices, local(): lax.all_to_all(chosen, 'req', split_axis=0, concat_axis=0, tiled=True)  4.11 us
    pallas_call x1, Pallas kernels, pick(): pl.pallas_call(pick_kernel, out_shape=jax.ShapeDtypeStruct((count, parts....  3.48 us
    reshape x3, local copies, waits for them, and re-layouts, by_step(): return a.reshape(a.shape[0], STEPS, PER_STEP).transpose(1, 0, 2)  3.06 us
  transfers between devices with their start and end apart: 3, of which 2 were waited for; matrix products, arithmetic and copies ran while one was open for 6% of the time, Pallas kernels for 11%

profile of v4, /device:TPU:13, one launch (start us, length us, event | category | flops | bytes accessed | tf_op | source)
XLA Modules:
  0.0 150.6 jit_solution(16106519762662239522)
XLA Ops:
  7.9 1.3 fusion.7
  11.1 1.7 %dynamic-slice_bitcast_fusion = bf16[16,8,8192]{2,1,0:T(8,128)(2,1)S(1)} fusion(bf16[3,128,8192]{2,1,0:T(8,128)(2,1)} %param.20, s32[]{:T(128)S(6)} %select_n.39), kind=kLoop, calls=%fused_computation | loop fusion | bytes 4194308 | tf_op jit(solution)/shard_map/reshape | solution.py:116
  12.9 1.5 %concatenate.3 = bf16[16,8,8320]{2,1,0:T(8,128)(2,1)} pad(bf16[16,8,8192]{2,1,0:T(8,128)(2,1)S(1)} %dynamic-slice_bitcast_fusion, bf16[]{:T(256)S(6)} %convert_element_type.26), padding=0_0x0_0x0_128 | pad | bytes 4227074 | tf_op jit(solution)/shard_map/concatenate | solution.py:119
  14.4 6.7 %all-to-all-start = ((bf16[16,8,8320]{2,1,0:T(8,128)(2,1)}), bf16[16,8,8320]{2,1,0:T(8,128)(2,1)S(1)}, u32[]{:S(2)}, u32[]{:S(2)}) async-start(bf16[16,8,8320]{2,1,0:T(8,128)(2,1)} %concatenate.3), calls=%async_computation | async-start | bytes 4259840 | tf_op jit(solution)/shard_map/all_to_all | solution.py:118
  21.1 0.0 all-gather.2.cloned.1.call-start
  21.2 0.7 pad.11
  21.8 54.7 %all-to-all-done.parts_ref = bf16[16,8,8320]{2,1,0:T(8,128)(2,1)S(1)} async-done(((bf16[16,8,8320]{2,1,0:T(8,128)(2,1)}), bf16[16,8,8320]{2,1,0:T(8,128)(2,1)S(1)}, u32[]{:S(2)}, u32[]{:S(2)}) %all-to-all-start) | async-done | bytes 2129952 | tf_op jit(solution)/shard_map/all_to_all | solution.py:118
  76.6 0.4 fusion.6
  77.0 0.2 select_reduce_fusion.index_ref
  77.2 3.5 %pick.1 = bf16[16,8,8192]{2,1,0:T(8,128)(2,1)S(1)} custom-call(s32[16]{0:T(128)S(1)} %select_reduce_fusion.index_ref, bf16[16,8,8320]{2,1,0:T(8,128)(2,1)S(1)} %all-to-all-done.parts_ref), custom_call_target="tpu_custom_call" | custom-call | tf_op jit(solution)/shard_map/pick/pallas_call | solution.py:32
  80.7 1.3 copy-done.1
  82.0 4.1 %all-to-all-start.1 = ((bf16[16,8,8192]{2,1,0:T(8,128)(2,1)}), bf16[16,8,8192]{2,1,0:T(8,128)(2,1)S(1)}, u32[]{:S(2)}, u32[]{:S(2)}) async-start(bf16[16,8,8192]{2,1,0:T(8,128)(2,1)} %copy-done.1), calls=%async_computation.1 | async-start | bytes 4194304 | tf_op jit(solution)/shard_map/all_to_all | solution.py:129
  86.1 0.6 dynamic_slice.19
  87.8 0.6 dynamic_slice.16
  89.1 0.1 copy.24
  89.2 0.1 compare_select_fusion
  89.4 0.3 fusion
  89.6 0.2 slice_reduce_fusion
  89.8 0.1 broadcast_in_dim.50
  89.9 0.7 broadcast_in_dim_reshape.7.elast_ref
  90.6 0.1 broadcast_in_dim.49
  90.7 0.7 broadcast_in_dim_reshape.6.skip_ref
  91.4 0.1 fusion.10
  91.6 1.0 copy.26
  92.6 1.0 copy.27
  93.6 1.0 copy.25
  95.2 0.9 select_bitcast_fusion
  96.1 0.8 pad_convert_fusion.tx_ref.tb_ref.tc_ref
  96.9 13.3 %local.1 = (f32[128,8192]{1,0:T(8,128)}, f32[128,8192]{1,0:T(8,128)}, bf16[128,512]{1,0:T(8,128)(2,1)}) custom-call(bf16[128,9216]{1,0:T(8,128)(2,1)} %xc_ref.1, bf16[128,9216]{1,0:T(8,128)(2,1)} %xc_ref.1, bf16[128,9216]{1,0:T(8,128)(2,1)} %xc_ref.1, f32[8,9216]{1,0:T(8,128)} %pad_convert_fusion.tx_ref.tb_ref.tc_ref, ...), custom_call_target="tpu_custom_call" | custom-call | flops 1000000000 | bytes 40000000 | tf_op jit(solution)/shard_map/local/pallas_call | solution.py:156
  110.3 23.3 %all-to-all-done.1 = bf16[16,8,8192]{2,1,0:T(8,128)(2,1)S(1)} async-done(((bf16[16,8,8192]{2,1,0:T(8,128)(2,1)}), bf16[16,8,8192]{2,1,0:T(8,128)(2,1)S(1)}, u32[]{:S(2)}, u32[]{:S(2)}) %all-to-all-start.1) | async-done | bytes 2097184 | tf_op jit(solution)/shard_map/all_to_all | solution.py:129
  133.5 1.4 copy-done.2
  134.9 8.9 %state.1 = (bf16[128,8192]{1,0:T(8,128)(2,1)}, bf16[1,128,8192]{2,1,0:T(8,128)(2,1)}) custom-call(s32[1]{0:T(128)S(6)} %convert_element_type.25.live_ref, bf16[128,8192]{1,0:T(8,128)(2,1)} %bitcast.26, f32[128,8192]{1,0:T(8,128)} %get-tuple-element.5.y_ref, f32[128,8192]{1,0:T(8,128)} %get-tuple-element.6.fresh_ref, ...), custom_call_target="tpu_custom_call" | custom-call | tf_op jit(solution)/shard_map/state/pallas_call | solution.py:173
  (25 shorter events, 0.1 us)
Async XLA Ops:
  7.2 13.9 %copy-start = (bf16[3,3,9216]{2,1,0:T(4,128)(2,1)S(1)}, bf16[3,3,9216]{2,1,0:T(4,128)(2,1)}, u32[]{:S(2)}) copy-start(bf16[3,3,9216]{2,1,0:T(4,128)(2,1)} %param.21) | copy-start | bytes 497668
  14.4 62.6 %copy-start.8 = (s32[16]{0:T(128)S(1)}, s32[16]{0:T(128)}, u32[]{:S(2)}) copy-start(s32[16]{0:T(128)} %param.22) | copy-start | bytes 196
  14.4 62.2 %all-to-all-start = ((bf16[16,8,8320]{2,1,0:T(8,128)(2,1)}), bf16[16,8,8320]{2,1,0:T(8,128)(2,1)S(1)}, u32[]{:S(2)}, u32[]{:S(2)}) async-start(bf16[16,8,8320]{2,1,0:T(8,128)(2,1)} %concatenate.3), calls=%async_computation | async-start | bytes 4259840 | tf_op jit(solution)/shard_map/all_to_all | solution.py:118
  21.1 74.1 %all-gather.2.cloned.1.call-start = ((), (), s32[]{:S(2)}) async-start(), calls=%async_computation.2 | async-start | bytes 1253376 | tf_op jit(solution)/shard_map/all_gather | solution.py:124
  80.6 1.3 copy-start.1
  82.0 5.9 %copy-start.9 = (s32[16]{0:T(128)S(1)}, s32[16]{0:T(128)}, u32[]{:S(2)}) copy-start(s32[16]{0:T(128)} %param.24) | copy-start | bytes 196
  82.0 7.1 %copy-start.5 = (f32[128,128]{1,0:T(8,128)S(1)}, f32[128,128]{1,0:T(8,128)}, u32[]{:S(2)}) copy-start(f32[128,128]{1,0:T(8,128)} %param.14) | copy-start | bytes 196612
  82.0 7.2 %copy-start.10 = (f32[128]{0:T(128)S(1)}, f32[128]{0:T(128)}, u32[]{:S(2)}) copy-start(f32[128]{0:T(128)} %param.18) | copy-start | bytes 1540
  82.0 7.2 %copy-start.6 = (f32[128]{0:T(128)S(1)}, f32[128]{0:T(128)}, u32[]{:S(2)}) copy-start(f32[128]{0:T(128)} %param.17) | copy-start | bytes 1540
  82.0 8.6 %copy-start.7 = (f32[128]{0:T(128)S(1)}, f32[128]{0:T(128)}, u32[]{:S(2)}) copy-start(f32[128]{0:T(128)} %param.19) | copy-start | bytes 1540
  82.0 51.5 %all-to-all-start.1 = ((bf16[16,8,8192]{2,1,0:T(8,128)(2,1)}), bf16[16,8,8192]{2,1,0:T(8,128)(2,1)S(1)}, u32[]{:S(2)}, u32[]{:S(2)}) async-start(bf16[16,8,8192]{2,1,0:T(8,128)(2,1)} %copy-done.1), calls=%async_computation.1 | async-start | bytes 4194304 | tf_op jit(solution)/shard_map/all_to_all | solution.py:129
  89.4 7.6 %copy-start.4 = (f32[128,128]{0,1:T(8,128)}, f32[128,128]{0,1:T(8,128)S(1)}, u32[]{:S(2)}) copy-start(f32[128,128]{0,1:T(8,128)S(1)} %compare_select_fusion) | copy-start | bytes 196612
  89.6 7.3 %copy-start.3 = (f32[128,128]{0,1:T(8,128)}, f32[128,128]{0,1:T(8,128)S(1)}, u32[]{:S(2)}) copy-start(f32[128,128]{0,1:T(8,128)S(1)} %fusion) | copy-start | bytes 196612
  133.5 1.4 copy-start.2
Sparse Core Ops, SparseCore 0:
  24.2 54.1 all-gather.1

commit v5 on v4

--- a/solution.py
+++ b/solution.py
@@ -113,15 +113,15 @@
     live = (hit_spans[mine] > 0).astype(jnp.int32)
     device = lax.axis_index("req")
     served = jnp.max(jnp.where(hit_owner == device, hit_slot, 0))
+    own_tail = lax.dynamic_slice_in_dim(cache_tails, served, 1, 0)
+    every_tail = lax.all_gather(own_tail, "req", axis=0, tiled=True)
     send = lax.dynamic_slice_in_dim(cache_states, served, 1, 0).reshape(count, NST // count, INNER)
     number = jnp.broadcast_to(mine.astype(send.dtype), send.shape[:2] + (128,))
+    send, every_tail = lax.optimization_barrier((jnp.concatenate([send, number], axis=2), every_tail))
     parts = lax.all_to_all(
-        jnp.concatenate([send, number], axis=2), "req", split_axis=0, concat_axis=0, tiled=True
+        send, "req", split_axis=0, concat_axis=0, tiled=True
     )
     every_request = parts[:, 0, INNER].astype(jnp.int32)
-    own_tail = lax.dynamic_slice_in_dim(cache_tails, served, 1, 0)
-    own_tail = jnp.pad(own_tail, ((0, 0), (0, 1), (0, 0)))
-    every_tail = lax.all_gather(own_tail, "req", axis=0, tiled=True)[:, :3]
     owners = jnp.sum(
         jnp.where(every_request[:, None] == jnp.arange(count)[None, :], hit_owner[None, :], 0), axis=1
     )

time: 151 us -> 151 us (level)
  blocking collectives: 0 us -> 77.7 us
  waiting for transfers between devices: 78.1 us -> 23.1 us
  between operations: 19.2 us -> 6.01 us
  starting transfers between devices: 10.8 us -> 6.01 us
  local copies, waits for them, and re-layouts: 12.8 us -> 9.53 us
    all_to_all x0 -> x1, blocking collectives: none -> 55.4 us  [local(): parts = lax.all_to_all(send, 'req', split_axis=0, concat_axis=0, tiled=True)]
    all_to_all x1 -> x0, waiting for transfers between devices: 54.7 us -> none  [local(): lax.all_to_all(jnp.concatenate([send, number], axis=2), 'req', split_axis...]
    all_gather x0 -> x1, blocking collectives: none -> 22.3 us  [local(): every_tail = lax.all_gather(own_tail, 'req', axis=0, tiled=True)]
    all_to_all x1 -> x0, starting transfers between devices: 6.69 us -> none  [local(): lax.all_to_all(jnp.concatenate([send, number], axis=2), 'req', split_axis...]
    all_to_all x1, starting transfers between devices: 4.11 us -> 6.01 us  [local(): lax.all_to_all(chosen, 'req', split_axis=0, concat_axis=0, tiled=True)]
  transfers between devices with their start and end apart: 3 -> 1, of which waited for: 2 -> 1; matrix products, arithmetic and copies ran while one was open for 6% -> 6% of each run, Pallas kernels for 11% -> 9%
where the time goes in v5:
time: 151 us
  blocking collectives  77.7 us (51%)
  Pallas kernels  24.2 us (16%)
  waiting for transfers between devices  23.1 us (15%)
  local copies, waits for them, and re-layouts  9.53 us (6%)
  starting transfers between devices  6.01 us (4%)
  between operations  6.01 us (4%)
  other arithmetic  3.81 us (3%)
    all_to_all x1, blocking collectives, local(): parts = lax.all_to_all(send, 'req', split_axis=0, concat_axis=0, tiled=True)  55.4 us
    all_to_all x1, waiting for transfers between devices, local(): lax.all_to_all(chosen, 'req', split_axis=0, concat_axis=0, tiled=True)  23.1 us
    all_gather x1, blocking collectives, local(): every_tail = lax.all_gather(own_tail, 'req', axis=0, tiled=True)  22.3 us
    pallas_call x1, Pallas kernels, local(): pl.pallas_call(local_kernel, grid=(STEPS,), out_shape=(jax.ShapeDtypeStru...  13.3 us
    pallas_call x1, Pallas kernels, local(): pl.pallas_call(state_kernel, grid=(STEPS,), out_shape=(jax.ShapeDtypeStru...  8.85 us
    all_to_all x1, starting transfers between devices, local(): lax.all_to_all(chosen, 'req', split_axis=0, concat_axis=0, tiled=True)  6.01 us
    reshape x3, local copies, waits for them, and re-layouts, by_step(): return a.reshape(a.shape[0], STEPS, PER_STEP).transpose(1, 0, 2)  3.07 us
  transfers between devices with their start and end apart: 1, of which 1 were waited for; matrix products, arithmetic and copies ran while one was open for 6% of the time, Pallas kernels for 9%

profile of v5, /device:TPU:13, one launch (start us, length us, event | category | flops | bytes accessed | tf_op | source)
XLA Modules:
  0.0 150.6 jit_solution(12255003845096037410)
XLA Ops:
  0.6 0.0 copy-start
  1.3 1.3 fusion.7
  4.6 22.3 %all_gather.3 = bf16[16,3,9216]{2,1,0:T(4,128)(2,1)} all-gather(bf16[1,3,9216]{2,1,0:T(4,128)(2,1)S(1)} %constant_dynamic-slice_fusion), channel_id=1, replica_groups=mesh['grp'=2,'req'=16] {'req'}, dimensions={0}, use_global_device_ids=true | all-gather | bytes 940032 | tf_op jit(solution)/shard_map/all_gather | solution.py:117
  27.0 1.8 %dynamic-slice_bitcast_fusion = bf16[16,8,8192]{2,1,0:T(8,128)(2,1)S(1)} fusion(bf16[3,128,8192]{2,1,0:T(8,128)(2,1)} %param.20, s32[]{:T(128)S(6)} %select_n.39), kind=kLoop, calls=%fused_computation | loop fusion | bytes 4194308 | tf_op jit(solution)/shard_map/reshape | solution.py:118
  28.8 0.2 concatenate.3
  28.9 0.0 copy-start.7
  28.9 55.4 %all_to_all.10.parts_ref = bf16[16,8,8320]{2,1,0:T(8,128)(2,1)S(1)} all-to-all(bf16[16,8,8320]{2,1,0:T(8,128)(2,1)S(1)} %concatenate.3), channel_id=1, replica_groups=mesh['grp'=2,'req'=16] {'req'}, dimensions={0} | all-to-all | bytes 4259840 | tf_op jit(solution)/shard_map/all_to_all | solution.py:121
  84.3 0.4 fusion.6
  84.7 0.2 select_reduce_fusion.index_ref
  84.9 2.0 %pick.1 = bf16[16,8,8192]{2,1,0:T(8,128)(2,1)} custom-call(s32[16]{0:T(128)S(1)} %select_reduce_fusion.index_ref, bf16[16,8,8320]{2,1,0:T(8,128)(2,1)S(1)} %all_to_all.10.parts_ref), custom_call_target="tpu_custom_call" | custom-call | tf_op jit(solution)/shard_map/pick/pallas_call | solution.py:32
  86.9 0.0 copy-start.8
  87.0 6.0 %all-to-all-start.1 = ((bf16[16,8,8192]{2,1,0:T(8,128)(2,1)}), bf16[16,8,8192]{2,1,0:T(8,128)(2,1)S(1)}, u32[]{:S(2)}, u32[]{:S(2)}) async-start(bf16[16,8,8192]{2,1,0:T(8,128)(2,1)} %pick.1), calls=%async_computation.1 | async-start | bytes 4194304 | tf_op jit(solution)/shard_map/all_to_all | solution.py:129
  93.0 0.6 dynamic_slice.19
  94.8 0.6 dynamic_slice.16
  96.1 0.1 copy.24
  96.2 0.1 compare_select_fusion
  96.3 0.3 fusion
  96.6 0.2 slice_reduce_fusion
  96.8 0.1 broadcast_in_dim.50
  96.9 0.7 broadcast_in_dim_reshape.7.elast_ref
  97.6 0.1 broadcast_in_dim.49
  97.7 0.7 broadcast_in_dim_reshape.6.skip_ref
  98.4 0.1 fusion.10
  98.5 1.1 copy.26
  99.6 1.0 copy.27
  100.6 1.0 copy.25
  102.2 0.9 select_bitcast_fusion
  103.2 0.8 pad_convert_fusion.tx_ref.tb_ref.tc_ref
  104.0 13.3 %local.1 = (f32[128,8192]{1,0:T(8,128)}, f32[128,8192]{1,0:T(8,128)}, bf16[128,512]{1,0:T(8,128)(2,1)}) custom-call(bf16[128,9216]{1,0:T(8,128)(2,1)} %xc_ref.1, bf16[128,9216]{1,0:T(8,128)(2,1)} %xc_ref.1, bf16[128,9216]{1,0:T(8,128)(2,1)} %xc_ref.1, f32[8,9216]{1,0:T(8,128)} %pad_convert_fusion.tx_ref.tb_ref.tc_ref, ...), custom_call_target="tpu_custom_call" | custom-call | flops 1000000000 | bytes 40000000 | tf_op jit(solution)/shard_map/local/pallas_call | solution.py:156
  117.3 23.1 %all-to-all-done.1 = bf16[16,8,8192]{2,1,0:T(8,128)(2,1)S(1)} async-done(((bf16[16,8,8192]{2,1,0:T(8,128)(2,1)}), bf16[16,8,8192]{2,1,0:T(8,128)(2,1)S(1)}, u32[]{:S(2)}, u32[]{:S(2)}) %all-to-all-start.1) | async-done | bytes 2097184 | tf_op jit(solution)/shard_map/all_to_all | solution.py:129
  140.4 1.4 copy-done.1
  141.8 8.9 %state.1 = (bf16[128,8192]{1,0:T(8,128)(2,1)}, bf16[1,128,8192]{2,1,0:T(8,128)(2,1)}) custom-call(s32[1]{0:T(128)S(6)} %convert_element_type.23.live_ref, bf16[128,8192]{1,0:T(8,128)(2,1)} %bitcast.25, f32[128,8192]{1,0:T(8,128)} %get-tuple-element.9.y_ref, f32[128,8192]{1,0:T(8,128)} %get-tuple-element.10.fresh_ref, ...), custom_call_target="tpu_custom_call" | custom-call | tf_op jit(solution)/shard_map/state/pallas_call | solution.py:173
  (19 shorter events, 0.1 us)
Async XLA Ops:
  0.6 4.0 %copy-start = (bf16[3,3,9216]{2,1,0:T(4,128)(2,1)S(1)}, bf16[3,3,9216]{2,1,0:T(4,128)(2,1)}, u32[]{:S(2)}) copy-start(bf16[3,3,9216]{2,1,0:T(4,128)(2,1)} %param.21) | copy-start | bytes 497668
  28.9 55.8 %copy-start.7 = (s32[16]{0:T(128)S(1)}, s32[16]{0:T(128)}, u32[]{:S(2)}) copy-start(s32[16]{0:T(128)} %param.22) | copy-start | bytes 196
  86.9 7.9 %copy-start.8 = (s32[16]{0:T(128)S(1)}, s32[16]{0:T(128)}, u32[]{:S(2)}) copy-start(s32[16]{0:T(128)} %param.24) | copy-start | bytes 196
  86.9 9.2 %copy-start.4 = (f32[128,128]{1,0:T(8,128)S(1)}, f32[128,128]{1,0:T(8,128)}, u32[]{:S(2)}) copy-start(f32[128,128]{1,0:T(8,128)} %param.14) | copy-start | bytes 196612
  86.9 9.3 %copy-start.9 = (f32[128]{0:T(128)S(1)}, f32[128]{0:T(128)}, u32[]{:S(2)}) copy-start(f32[128]{0:T(128)} %param.18) | copy-start | bytes 1540
  86.9 9.3 %copy-start.5 = (f32[128]{0:T(128)S(1)}, f32[128]{0:T(128)}, u32[]{:S(2)}) copy-start(f32[128]{0:T(128)} %param.17) | copy-start | bytes 1540
  86.9 10.7 %copy-start.6 = (f32[128]{0:T(128)S(1)}, f32[128]{0:T(128)}, u32[]{:S(2)}) copy-start(f32[128]{0:T(128)} %param.19) | copy-start | bytes 1540
  87.0 53.5 %all-to-all-start.1 = ((bf16[16,8,8192]{2,1,0:T(8,128)(2,1)}), bf16[16,8,8192]{2,1,0:T(8,128)(2,1)S(1)}, u32[]{:S(2)}, u32[]{:S(2)}) async-start(bf16[16,8,8192]{2,1,0:T(8,128)(2,1)} %pick.1), calls=%async_computation.1 | async-start | bytes 4194304 | tf_op jit(solution)/shard_map/all_to_all | solution.py:129
  96.3 7.6 %copy-start.3 = (f32[128,128]{0,1:T(8,128)}, f32[128,128]{0,1:T(8,128)S(1)}, u32[]{:S(2)}) copy-start(f32[128,128]{0,1:T(8,128)S(1)} %compare_select_fusion) | copy-start | bytes 196612
  96.6 7.4 %copy-start.2 = (f32[128,128]{0,1:T(8,128)}, f32[128,128]{0,1:T(8,128)S(1)}, u32[]{:S(2)}) copy-start(f32[128,128]{0,1:T(8,128)S(1)} %fusion) | copy-start | bytes 196612
  140.4 1.4 copy-start.1

commit v6 on v5

--- a/solution.py
+++ b/solution.py
@@ -179,7 +179,7 @@
         ),
         in_specs=[pl.BlockSpec(memory_space=pltpu.SMEM), wide(NST), wide(rows), wide(NST), group, tall, wide(1)],
         out_specs=(wide(rows), pl.BlockSpec((1, NST, COLS), lambda i: (0, 0, i))),
-        compiler_params=pltpu.CompilerParams(vmem_limit_bytes=58 * 2**20),
+        compiler_params=pltpu.CompilerParams(vmem_limit_bytes=14 * 2**20),
         name="state",
     )(live[None], start, y_local, fresh, c_part, by_step(jnp.exp(cum)), elast)
 

time: 151 us -> 152 us (level)
  Pallas kernels: 24.2 us -> 20.6 us
  local copies, waits for them, and re-layouts: 9.53 us -> 12 us
  waiting for transfers between devices: 23.1 us -> 24.8 us
    unnamed x21 -> x25, local copies, waits for them, and re-layouts: 1.51 us -> 5.42 us
    pallas_call x1, Pallas kernels: 8.85 us -> 5.3 us  [local(): pl.pallas_call(state_kernel, grid=(STEPS,), out_shape=(jax.ShapeDtypeStru...]
    all_to_all x1, waiting for transfers between devices: 23.1 us -> 24.8 us  [local(): lax.all_to_all(chosen, 'req', split_axis=0, concat_axis=0, tiled=True)]
  transfers between devices with their start and end apart: 1 -> 1, of which waited for: 1 -> 1; matrix products, arithmetic and copies ran while one was open for 6% -> 5% of each run, Pallas kernels for 9% -> 9%
where the time goes in v6:
time: 152 us; the launch traced here: 151 us
  blocking collectives  77.7 us (51%)
  waiting for transfers between devices  24.8 us (16%)
  Pallas kernels  20.6 us (14%)
  local copies, waits for them, and re-layouts  12 us (8%)
  starting transfers between devices  6.01 us (4%)
  between operations  5.86 us (4%)
  other arithmetic  3.81 us (3%)
    all_to_all x1, blocking collectives, local(): parts = lax.all_to_all(send, 'req', split_axis=0, concat_axis=0, tiled=True)  55.4 us
    all_to_all x1, waiting for transfers between devices, local(): lax.all_to_all(chosen, 'req', split_axis=0, concat_axis=0, tiled=True)  24.8 us
    all_gather x1, blocking collectives, local(): every_tail = lax.all_gather(own_tail, 'req', axis=0, tiled=True)  22.3 us
    pallas_call x1, Pallas kernels, local(): pl.pallas_call(local_kernel, grid=(STEPS,), out_shape=(jax.ShapeDtypeStru...  13.3 us
    all_to_all x1, starting transfers between devices, local(): lax.all_to_all(chosen, 'req', split_axis=0, concat_axis=0, tiled=True)  6.01 us
    unnamed x25, local copies, waits for them, and re-layouts  5.42 us
    pallas_call x1, Pallas kernels, local(): pl.pallas_call(state_kernel, grid=(STEPS,), out_shape=(jax.ShapeDtypeStru...  5.3 us
  transfers between devices with their start and end apart: 1, of which 1 were waited for; matrix products, arithmetic and copies ran while one was open for 5% of the time, Pallas kernels for 9%

profile of v6, /device:TPU:13, one launch (start us, length us, event | category | flops | bytes accessed | tf_op | source)
XLA Modules:
  0.0 151.0 jit_solution(6702942082039653489)
XLA Ops:
  0.6 0.0 copy-start
  1.3 1.3 fusion.7
  4.6 22.3 %all_gather.3 = bf16[16,3,9216]{2,1,0:T(4,128)(2,1)} all-gather(bf16[1,3,9216]{2,1,0:T(4,128)(2,1)S(1)} %constant_dynamic-slice_fusion), channel_id=1, replica_groups=mesh['grp'=2,'req'=16] {'req'}, dimensions={0}, use_global_device_ids=true | all-gather | bytes 940032 | tf_op jit(solution)/shard_map/all_gather | solution.py:117
  27.0 1.8 %dynamic-slice_bitcast_fusion = bf16[16,8,8192]{2,1,0:T(8,128)(2,1)S(1)} fusion(bf16[3,128,8192]{2,1,0:T(8,128)(2,1)} %param.20, s32[]{:T(128)S(6)} %select_n.39), kind=kLoop, calls=%fused_computation | loop fusion | bytes 4194308 | tf_op jit(solution)/shard_map/reshape | solution.py:118
  28.8 0.2 concatenate.3
  28.9 55.4 %all_to_all.10.parts_ref = bf16[16,8,8320]{2,1,0:T(8,128)(2,1)S(1)} all-to-all(bf16[16,8,8320]{2,1,0:T(8,128)(2,1)S(1)} %concatenate.3), channel_id=1, replica_groups=mesh['grp'=2,'req'=16] {'req'}, dimensions={0} | all-to-all | bytes 4259840 | tf_op jit(solution)/shard_map/all_to_all | solution.py:121
  84.3 0.4 fusion.6
  84.7 0.2 select_reduce_fusion.index_ref
  84.9 2.0 %pick.1 = bf16[16,8,8192]{2,1,0:T(8,128)(2,1)} custom-call(s32[16]{0:T(128)S(1)} %select_reduce_fusion.index_ref, bf16[16,8,8320]{2,1,0:T(8,128)(2,1)S(1)} %all_to_all.10.parts_ref), custom_call_target="tpu_custom_call" | custom-call | tf_op jit(solution)/shard_map/pick/pallas_call | solution.py:32
  87.0 6.0 %all-to-all-start.1 = ((bf16[16,8,8192]{2,1,0:T(8,128)(2,1)}), bf16[16,8,8192]{2,1,0:T(8,128)(2,1)S(1)}, u32[]{:S(2)}, u32[]{:S(2)}) async-start(bf16[16,8,8192]{2,1,0:T(8,128)(2,1)} %pick.1), calls=%async_computation.1 | async-start | bytes 4194304 | tf_op jit(solution)/shard_map/all_to_all | solution.py:129
  93.0 0.6 dynamic_slice.19
  94.7 0.6 dynamic_slice.16
  95.9 0.1 copy.24
  96.1 0.1 compare_select_fusion
  96.2 0.3 fusion
  96.5 0.2 slice_reduce_fusion
  96.7 0.1 broadcast_in_dim.50
  96.7 0.1 broadcast_in_dim_reshape.7.elast_ref
  96.9 0.1 broadcast_in_dim.49
  96.9 0.7 broadcast_in_dim_reshape.6.skip_ref
  97.7 0.1 fusion.10
  97.8 1.1 copy.26
  98.8 0.2 copy.27
  99.0 1.0 copy.25
  100.6 0.9 select_bitcast_fusion
  101.5 0.8 pad_convert_fusion.tx_ref.tb_ref.tc_ref
  102.3 13.3 %local.1 = (f32[128,8192]{1,0:T(8,128)}, f32[128,8192]{1,0:T(8,128)}, bf16[128,512]{1,0:T(8,128)(2,1)}) custom-call(bf16[128,9216]{1,0:T(8,128)(2,1)} %xc_ref.1, bf16[128,9216]{1,0:T(8,128)(2,1)} %xc_ref.1, bf16[128,9216]{1,0:T(8,128)(2,1)} %xc_ref.1, f32[8,9216]{1,0:T(8,128)} %pad_convert_fusion.tx_ref.tb_ref.tc_ref, ...), custom_call_target="tpu_custom_call" | custom-call | flops 1000000000 | bytes 40000000 | tf_op jit(solution)/shard_map/local/pallas_call | solution.py:156
  115.7 24.8 %all-to-all-done.1 = bf16[16,8,8192]{2,1,0:T(8,128)(2,1)S(1)} async-done(((bf16[16,8,8192]{2,1,0:T(8,128)(2,1)}), bf16[16,8,8192]{2,1,0:T(8,128)(2,1)S(1)}, u32[]{:S(2)}, u32[]{:S(2)}) %all-to-all-start.1) | async-done | bytes 2097184 | tf_op jit(solution)/shard_map/all_to_all | solution.py:129
  140.4 2.2 %copy-done.1 = f32[128,8192]{1,0:T(8,128)S(1)} copy-done((f32[128,8192]{1,0:T(8,128)S(1)}, f32[128,8192]{1,0:T(8,128)}, u32[]{:S(2)}) %copy-start.1) | copy-done | bytes 4194328
  142.6 2.2 %copy-done.2 = f32[128,8192]{1,0:T(8,128)S(1)} copy-done((f32[128,8192]{1,0:T(8,128)S(1)}, f32[128,8192]{1,0:T(8,128)}, u32[]{:S(2)}) %copy-start.2) | copy-done | bytes 4194328
  144.8 0.9 copy-done.3
  145.7 5.3 %state.1 = (bf16[128,8192]{1,0:T(8,128)(2,1)}, bf16[1,128,8192]{2,1,0:T(8,128)(2,1)}) custom-call(s32[1]{0:T(128)S(6)} %convert_element_type.23.live_ref, bf16[128,8192]{1,0:T(8,128)(2,1)S(1)} %bitcast.25, f32[128,8192]{1,0:T(8,128)S(1)} %copy-done.1, f32[128,8192]{1,0:T(8,128)S(1)} %copy-done.2, bf16[128,512]{1,0:T(8,128)(2,1)S(1)} %copy-done.3, ...), custom_call_target="tpu_custom_call" | custom-call | tf_op jit(solution)/shard_map/state/pallas_call | solution.py:173
  (23 shorter events, 0.1 us)
Async XLA Ops:
  0.6 4.0 %copy-start = (bf16[3,3,9216]{2,1,0:T(4,128)(2,1)S(1)}, bf16[3,3,9216]{2,1,0:T(4,128)(2,1)}, u32[]{:S(2)}) copy-start(bf16[3,3,9216]{2,1,0:T(4,128)(2,1)} %param.21) | copy-start | bytes 497668
  28.9 55.8 %copy-start.9 = (s32[16]{0:T(128)S(1)}, s32[16]{0:T(128)}, u32[]{:S(2)}) copy-start(s32[16]{0:T(128)} %param.22) | copy-start | bytes 196
  86.9 7.8 %copy-start.10 = (s32[16]{0:T(128)S(1)}, s32[16]{0:T(128)}, u32[]{:S(2)}) copy-start(s32[16]{0:T(128)} %param.24) | copy-start | bytes 196
  86.9 9.0 %copy-start.6 = (f32[128,128]{1,0:T(8,128)S(1)}, f32[128,128]{1,0:T(8,128)}, u32[]{:S(2)}) copy-start(f32[128,128]{1,0:T(8,128)} %param.14) | copy-start | bytes 196612
  86.9 9.1 %copy-start.11 = (f32[128]{0:T(128)S(1)}, f32[128]{0:T(128)}, u32[]{:S(2)}) copy-start(f32[128]{0:T(128)} %param.18) | copy-start | bytes 1540
  86.9 9.1 %copy-start.7 = (f32[128]{0:T(128)S(1)}, f32[128]{0:T(128)}, u32[]{:S(2)}) copy-start(f32[128]{0:T(128)} %param.17) | copy-start | bytes 1540
  86.9 9.9 %copy-start.8 = (f32[128]{0:T(128)S(1)}, f32[128]{0:T(128)}, u32[]{:S(2)}) copy-start(f32[128]{0:T(128)} %param.19) | copy-start | bytes 1540
  87.0 53.5 %all-to-all-start.1 = ((bf16[16,8,8192]{2,1,0:T(8,128)(2,1)}), bf16[16,8,8192]{2,1,0:T(8,128)(2,1)S(1)}, u32[]{:S(2)}, u32[]{:S(2)}) async-start(bf16[16,8,8192]{2,1,0:T(8,128)(2,1)} %pick.1), calls=%async_computation.1 | async-start | bytes 4194304 | tf_op jit(solution)/shard_map/all_to_all | solution.py:129
  96.2 6.1 %copy-start.5 = (f32[128,128]{0,1:T(8,128)}, f32[128,128]{0,1:T(8,128)S(1)}, u32[]{:S(2)}) copy-start(f32[128,128]{0,1:T(8,128)S(1)} %compare_select_fusion) | copy-start | bytes 196612
  96.5 5.9 %copy-start.4 = (f32[128,128]{0,1:T(8,128)}, f32[128,128]{0,1:T(8,128)S(1)}, u32[]{:S(2)}) copy-start(f32[128,128]{0,1:T(8,128)S(1)} %fusion) | copy-start | bytes 196612
  140.4 2.2 %copy-start.1 = (f32[128,8192]{1,0:T(8,128)S(1)}, f32[128,8192]{1,0:T(8,128)}, u32[]{:S(2)}) copy-start(f32[128,8192]{1,0:T(8,128)} %get-tuple-element.9.y_ref) | copy-start | bytes 12582916
  142.6 2.2 %copy-start.2 = (f32[128,8192]{1,0:T(8,128)S(1)}, f32[128,8192]{1,0:T(8,128)}, u32[]{:S(2)}) copy-start(f32[128,8192]{1,0:T(8,128)} %get-tuple-element.10.fresh_ref) | copy-start | bytes 12582916
  144.8 0.9 copy-start.3
